TPU v7x, 32 devices: a whole 2x2x4 slice. The times are simulated.
32 devices in a mesh: batch: 2 (over y), freq: 8 (over z, x), elem: 2 (over core).
Axes of the slice: x: 2, y: 2, z: 4, core: 2. Of those that a mesh axis runs over, the one named last changes fastest.
Arguments:
- flaw_cells: int32 [512], P('batch'), parts along dimension 0, may hold values from 0 to 255, each once
- flaw_blocks: int32 [16], P('batch'), parts along dimension 0, may hold values from 0 to 7, each once
- element_channel: int32 [256], P('elem'), may hold values from 0 to 255, each once
- focal_delay: float32 [256, 256], replicated, may hold values from 0 to 64
- beam_field: bfloat16 [128, 2, 256, 256], P('freq', None, 'elem'), may hold values from -0.125 to 0.125
- flaw_size: float32 [4, 128], P('batch'), parts along dimension 0, may hold values from 0.5 to 4
- flaw_slope: float32 [4, 128], P('batch'), parts along dimension 0, may hold values from 0.2 to 1
- noise_level: float32 [4, 128], P(('batch', 'elem'), 'freq'), parts along dimension 0, may hold values from 0.5 to 5
Outputs:
- flaw_peak: float32 [4, 128], P(('batch', 'elem'), 'freq'), parts along dimension 0
- detection: float32 [4, 128], P(('batch', 'elem'), 'freq'), parts along dimension 0
There are 2 independent parts, one for each index of `batch`. A program takes and returns all parts, laid end to end along the dimension named above; an argument that names none is the same for every part. Nothing has to cross between parts.
Inputs may be any that keep to these rules, and one draw needn't show every extreme that they name: `flaw_cells`: every site holds exactly one flaw. `flaw_blocks`: every scan block belongs to exactly one flaw group. `element_channel`: every channel drives exactly one element.
All inputs are finite; a program needn't handle non-finite values.
Results may differ from a plain program's by a relative error of at most 0.0011.
Values may be sent and summed in bfloat16 or wider, within the bound.
No kernel may reach another device: no remote copies, remote signals or barrier semaphores. Data moves between devices by JAX's collectives and lax.ppermute only.
A program may use at most 64 MiB of HBM per device.

v0:
```python
import math

import jax
import jax.numpy as jnp
from jax import lax
from jax.sharding import PartitionSpec as P

W_DEV = 16
FG = 128
NB = 4
SB = 32
T_CAP = 1024


EDGE = 0.6
STEEP = 3.0
EPS = 1e-05


def kirchhoff(angular, flaw_size, flaw_slope):
    angles = angular[None, :, None] * (2.0 * flaw_size * flaw_slope)[:, None, :]
    real_part = flaw_size[:, None, :] * (1.0 + EDGE) * jnp.cos(angles)
    imag_part = flaw_size[:, None, :] * (EDGE - 1.0) * jnp.sin(angles)
    return (real_part, imag_part)


def focal_law(angular, delays):
    phases = angular[:, None, None, None] * delays[None]
    return jnp.concatenate([jnp.cos(phases), -jnp.sin(phases)], axis=-1).astype(jnp.bfloat16)


def field_matrix(fields):
    real_part = fields[:, 0]
    imag_part = fields[:, 1]
    upper_rows = jnp.concatenate([real_part, imag_part], axis=-1)
    lower_rows = jnp.concatenate([-imag_part, real_part], axis=-1)
    return jnp.concatenate([upper_rows, lower_rows], axis=1)


def combine(product, k_real, k_imag):
    columns = k_real.shape[-1]
    real_part = product[..., :columns]
    imag_part = product[..., columns:]
    scale_real = k_real[:, :, None, :]
    scale_imag = k_imag[:, :, None, :]
    return jnp.stack(
        [
            scale_real * real_part - scale_imag * imag_part,
            scale_real * imag_part + scale_imag * real_part,
        ],
        axis=2,
    )


def envelope_peak(spectra, row_count):
    groups, freq_total, planes, columns = spectra.shape
    sample_count = min(T_CAP, 2 * freq_total)
    time_block = min(128, sample_count)
    freq_index = jnp.arange(freq_total, dtype=jnp.int32)
    scaling = 1.0 / math.sqrt(freq_total)

    def advance(step_index, running):
        sample_times = step_index * time_block + jnp.arange(time_block, dtype=jnp.int32)
        phase_steps = freq_index[:, None] * sample_times[None, :] % (2 * freq_total)
        angles = phase_steps.astype(jnp.float32) * (math.pi / freq_total)
        cosine = jnp.cos(angles)
        sine_part = jnp.sin(angles)
        twiddle = jnp.stack(
            [jnp.stack([cosine, sine_part], axis=1), jnp.stack([-sine_part, cosine], axis=1)],
            axis=1,
        )
        twiddle_high = lax.optimization_barrier(twiddle.astype(jnp.bfloat16))
        twiddle_low = (twiddle - twiddle_high.astype(jnp.float32)).astype(jnp.bfloat16)
        signal = jnp.einsum(
            "gwcx,wckt->gkxt", spectra, twiddle_high, preferred_element_type=jnp.float32
        )
        signal = signal + jnp.einsum(
            "gwcx,wckt->gkxt", spectra, twiddle_low, preferred_element_type=jnp.float32
        )
        signal = signal * scaling
        magnitude = jnp.sqrt(signal[:, 0] * signal[:, 0] + signal[:, 1] * signal[:, 1])
        magnitude = magnitude.reshape(groups, row_count, columns // row_count, time_block)
        return jnp.maximum(running, jnp.max(magnitude, axis=(1, 3)))

    initial = jnp.zeros((groups, columns // row_count), jnp.float32)
    return lax.fori_loop(0, sample_count // time_block, advance, initial)


def regroup_peaks(moved):
    groups, freq_total, planes, row_count, flaw_count = moved.shape
    return envelope_peak(
        moved.reshape(groups, freq_total, planes, row_count * flaw_count), row_count
    )


def body(
    flaw_cells,
    flaw_blocks,
    element_channel,
    focal_delay,
    beam_field,
    flaw_size,
    flaw_slope,
    noise_level,
):
    freq_count = lax.axis_size("freq")
    freq_total = W_DEV * freq_count
    group_total = flaw_size.shape[0]
    row_total = NB * SB
    first_freq = lax.axis_index("freq") * W_DEV
    angular = (first_freq + jnp.arange(W_DEV, dtype=jnp.int32)).astype(jnp.float32) * (
        math.pi / freq_total
    )
    scan_rows = (
        flaw_blocks.reshape(group_total, NB)[:, :, None] * SB
        + jnp.arange(SB, dtype=jnp.int32)[None, None, :]
    ).reshape(group_total, row_total)
    delays = jnp.moveaxis(
        jnp.take(jnp.take(focal_delay, element_channel, axis=0), scan_rows, axis=1), 0, 2
    )
    fields = jnp.take(beam_field, flaw_cells, axis=3).reshape(
        W_DEV, 2, element_channel.shape[0], group_total, FG
    )
    k_real, k_imag = kirchhoff(angular, flaw_size, flaw_slope)
    focal_terms = focal_law(angular, delays)
    field_terms = field_matrix(fields)
    product = jnp.einsum(
        "wgre,wegf->gwrf", focal_terms, field_terms, preferred_element_type=jnp.float32
    )
    partial_value = combine(product, k_real, k_imag).astype(jnp.bfloat16)
    rounded_term = lax.optimization_barrier(partial_value).astype(jnp.float32)
    summed = lax.psum_scatter(
        rounded_term.astype(jnp.bfloat16), "elem", scatter_dimension=0, tiled=True
    )
    partial_peak = regroup_peaks(
        lax.all_to_all(summed, "freq", split_axis=3, concat_axis=1, tiled=True)
    )
    whole_peak = lax.pmax(partial_peak, "freq")
    columns = FG // freq_count
    flaw_peak = lax.dynamic_slice_in_dim(whole_peak, lax.axis_index("freq") * columns, columns, 1)
    detection = jax.nn.sigmoid(STEEP * (jnp.log(flaw_peak + EPS) - jnp.log(noise_level)))
    return (flaw_peak, detection)


def solution(mesh):
    in_specs = (
        P("batch"),
        P("batch"),
        P("elem"),
        P(),
        P("freq", None, "elem", None),
        P("batch", None),
        P("batch", None),
        P(("batch", "elem"), "freq"),
    )
    out_specs = (P(("batch", "elem"), "freq"), P(("batch", "elem"), "freq"))
    return jax.shard_map(body, mesh=mesh, in_specs=in_specs, out_specs=out_specs, check_vma=False)
```

profile of v0, /device:TPU:0, one launch (start us, length us, event | category | flops | bytes accessed | tf_op | source)
XLA Modules:
  0.0 130.7 jit_solution(10028995258592045228)
XLA Ops:
  7.2 0.0 copy-start
  7.2 0.0 all-reduce.3.cloned.1.call-start
  7.2 0.7 compare_select_fusion.3
  7.9 1.2 compare_and_fusion
  9.1 0.7 broadcast_multiply_fusion.2
  9.7 0.1 mul.298
  9.8 0.1 add.209
  9.9 0.1 add.219
  10.0 0.1 add.210
  10.1 0.7 compare_select_fusion
  10.8 0.7 and_bitcast_fusion
  11.4 3.5 %copy.28 = bf16[16,2,128,256]{2,0,3,1:T(8,128)(2,1)S(1)} copy(bf16[16,2,128,256]{3,2,1,0:T(8,128)(2,1)} %param.14) | data formatting | bytes 4194304 | tf_op args[4]
  14.9 2.3 %gather_fusion.2 = bf16[256,16,2,128]{3,1,2,0:T(8,128)(2,1)} fusion(bf16[16,2,128,256]{2,0,3,1:T(8,128)(2,1)S(1)} %copy.28, s32[1024]{0:T(1024)S(1)} %pad_clamp_fusion), kind=kCustom, calls=%fused_computation.2 | custom fusion | bytes 4195328 | tf_op jit(solution)/shard_map/jit(_take)/gather | solution.py:121
  17.2 3.5 %copy.30 = bf16[16,2,128,2,128]{4,2,0,3,1:T(8,128)(2,1)S(1)} copy(bf16[16,2,128,2,128]{2,0,1,4,3:T(8,128)(2,1)} %bitcast.85) | data formatting | bytes 4194304 | tf_op jit(solution)/shard_map/jit(_take)/gather | solution.py:121
  20.7 0.2 broadcast_select_fusion.1
  20.9 0.1 slice_bitcast_fusion
  21.0 0.1 fusion.42
  21.2 0.1 add.212
  21.3 0.0 copy-done
  21.3 0.8 gather_fusion
  22.1 1.4 %broadcast_select_fusion.3 = f32[128,256]{1,0:T(8,128)} fusion(f32[128,256]{1,0:T(8,128)S(1)} %gather_fusion, pred[128]{0:T(512)(128)(4,1)} %compare_and_fusion), kind=kLoop, calls=%fused_computation.64 | loop fusion | flops 32768 | bytes 262272 | tf_op jit(solution)/shard_map/jit(_take)/select_n | solution.py:119
  23.5 1.0 copy.27
  24.5 0.5 compare_and_fusion.1
  25.0 1.3 %gather_fusion.1 = f32[256,128]{1,0:T(8,128)} fusion(f32[128,256]{0,1:T(8,128)S(1)} %copy.27, s32[1024]{0:T(1024)S(1)} %pad_clamp_fusion.1), kind=kCustom, calls=%fused_computation.1 | custom fusion | bytes 263168 | tf_op jit(solution)/shard_map/jit(_take)/gather | solution.py:119
  26.3 1.0 broadcast_select_fusion.2
  27.3 7.8 %fusion.30 = (bf16[16,2,128,128]{3,2,0,1:T(8,128)(2,1)S(1)}, bf16[16,2,128,128]{3,2,0,1:T(8,128)(2,1)S(1)}) fusion(f32[2,128,128]{2,1,0:T(8,128)S(1)} %broadcast_select_fusion.2, f32[16]{0:T(128)S(1)} %convert_multiply_fusion), kind=kLoop, calls=%fused_computation.49 | loop fusion | flops 2097152 | bytes 2228288 | tf_op jit(solution)/shard_map/convert.4
  35.2 0.7 broadcast_multiply_fusion.1
  35.9 0.1 fusion.38
  36.0 1.4 %fusion.22 = f32[2,16,128,256]{3,2,1,0:T(8,128)S(1)} fusion(bf16[16,128,2,128]{3,1,0,2:T(8,128)(2,1)S(1)} %get-tuple-element.144, bf16[16,128,2,128]{3,1,0,2:T(8,128)(2,1)S(1)} %fusion.42, bf16[16,128,2,128]{3,1,0,2:T(8,128)(2,1)S(1)} %get-tuple-element.143, bf16[16,2,128,128]{3,2,0,1:T(8,128)(2,1)S(1)} %get-tuple-element.146, ...), kind=kOutput, calls=%fused_computation.39 | convolution fusion | flops 557842432 | bytes 9437184 | tf_op jit(solution)/shard_map/wgre,wegf->gwrf/dot_general | solution.py:127
  37.4 0.6 fusion.36
  38.1 1.5 %pad_maximum_fusion.1 = bf16[2,16,2,128,128]{4,3,1,0,2:T(8,128)(2,1)} fusion(bf16[2,16,1,128,128]{4,3,1,0,2:T(8,128)(2,1)S(1)} %get-tuple-element.142, bf16[2,16,1,128,128]{4,3,1,0,2:T(8,128)(2,1)S(1)} %get-tuple-element.141), kind=kLoop, calls=%fused_computation.55 | loop fusion | flops 1048576 | bytes 4194304 | tf_op jit(solution)/shard_map/stack | solution.py:46
  39.5 0.0 copy-start.2
  39.5 0.0 all-reduce.3.cloned.1.call-update
  39.6 0.6 copy-done.2
  40.2 0.6 dynamic-slice
  40.8 22.9 %all-reduce.3.cloned.1.call-done = bf16[2,16,2,128,128]{4,3,1,0,2:T(8,128)(2,1)} async-done(((bf16[2,16,2,128,128]{4,3,1,0,2:T(8,128)(2,1)}), bf16[2,16,2,128,128]{4,3,1,0,2:T(8,128)(2,1)}) %all-reduce.3.cloned.1.call-update) | async-done | bytes 2097168
  63.6 1.9 %constant_dynamic-slice_fusion = bf16[1,16,2,128,128]{4,3,1,0,2:T(8,128)(2,1)S(1)} fusion(bf16[2,16,2,128,128]{4,3,1,0,2:T(8,128)(2,1)} %all-reduce.3.cloned.1.call-done, u32[]{:T(128)} %bitcast.34), kind=kLoop, calls=%fused_computation.81 | loop fusion | bytes 2097156
  65.6 1.7 %copy.31 = bf16[1,16,2,128,128]{4,1,0,2,3:T(8,128)(2,1)} copy(bf16[1,16,2,128,128]{4,3,1,0,2:T(8,128)(2,1)S(1)} %constant_dynamic-slice_fusion) | data formatting | bytes 2097152 | tf_op jit(solution)/shard_map/reduce_scatter | solution.py:132
  67.2 5.8 %all-to-all-start = ((bf16[1,16,2,128,128]{4,1,0,2,3:T(8,128)(2,1)}), bf16[1,16,2,128,128]{4,1,0,2,3:T(8,128)(2,1)S(1)}, u32[]{:S(2)}, u32[]{:S(2)}) async-start(bf16[1,16,2,128,128]{4,1,0,2,3:T(8,128)(2,1)} %copy.31), calls=%async_computation | async-start | bytes 2097152 | tf_op jit(solution)/shard_map/all_to_all | solution.py:136
  73.0 26.2 %all-to-all-done = bf16[1,16,2,128,128]{4,1,0,2,3:T(8,128)(2,1)S(1)} async-done(((bf16[1,16,2,128,128]{4,1,0,2,3:T(8,128)(2,1)}), bf16[1,16,2,128,128]{4,1,0,2,3:T(8,128)(2,1)S(1)}, u32[]{:S(2)}, u32[]{:S(2)}) %all-to-all-start) | async-done | bytes 1048608 | tf_op jit(solution)/shard_map/all_to_all | solution.py:136
  99.2 0.4 copy.32
  99.7 0.5 reshape.333
  100.2 0.0 copy-start.1
  100.2 3.5 %while.16 = (s32[]{:T(128)}, f32[1,128]{1,0:T(1,128)S(1)}, bf16[1,128,2,2048]{3,1,2,0:T(8,128)(2,1)S(1)}, s32[]{:T(128)}, s32[]{:T(128)}, /*index=5*/s32[]{:T(128)}) while((s32[]{:T(128)}, f32[1,128]{1,0:T(1,128)S(1)}, bf16[1,128,2,2048]{3,1,2,0:T(8,128)(2,1)S(1)}, s32[]{:T(128)}, s32[]{:T(128)}, /*index=5*/s32[]{:T(128)}) %tuple.58), condition=%wide.region_4.5_spmd.clone, body=%wide.region_1.4_spmd.clone.sunk | while | flops 539607296 | bytes 12078175 | solution.py:86
  100.2 0.3 fusion.55
  100.6 0.4 convolution_bitcast_fusion.3
  101.0 0.5 fusion.57
  101.5 0.4 fusion.58
  102.0 0.3 fusion.55
  102.4 0.4 convolution_bitcast_fusion.3
  102.8 0.5 fusion.57
  103.3 0.4 fusion.58
  103.7 19.5 %pmax.7 = f32[1,128]{1,0:T(1,128)S(1)} all-reduce(f32[1,128]{1,0:T(1,128)S(1)} %get-tuple-element.113), channel_id=1, replica_groups=mesh['batch'=2,'freq'=8,'elem'=2] {'freq'}, use_global_device_ids=true, to_apply=%region_5.6 | all-reduce | flops 128 | bytes 1024 | tf_op jit(solution)/shard_map/pmax | solution.py:138
  123.2 0.0 copy-done.1
  123.2 0.6 add_divide_fusion
  (17 shorter events, 0.2 us)
Async XLA Ops:
  7.2 14.2 %copy-start = (f32[256,256]{1,0:T(8,128)S(1)}, f32[256,256]{1,0:T(8,128)}, u32[]{:S(2)}) copy-start(f32[256,256]{1,0:T(8,128)} %param.13) | copy-start | bytes 786436
  7.2 56.5 %all-reduce.3.cloned.1.call-start = ((), (), s32[]{:S(2)}) async-start(), calls=%async_computation.1 | async-start | bytes 4194304
  39.5 0.7 copy-start.2
  67.2 32.0 %all-to-all-start = ((bf16[1,16,2,128,128]{4,1,0,2,3:T(8,128)(2,1)}), bf16[1,16,2,128,128]{4,1,0,2,3:T(8,128)(2,1)S(1)}, u32[]{:S(2)}, u32[]{:S(2)}) async-start(bf16[1,16,2,128,128]{4,1,0,2,3:T(8,128)(2,1)} %copy.31), calls=%async_computation | async-start | bytes 2097152 | tf_op jit(solution)/shard_map/all_to_all | solution.py:136
  100.2 23.0 %copy-start.1 = (f32[1,16]{1,0:T(1,128)S(1)}, f32[1,16]{1,0:T(1,128)}, u32[]{:S(2)}) copy-start(f32[1,16]{1,0:T(1,128)} %param.17) | copy-start | bytes 196
Sparse Core Ops, SparseCore 0:
  39.7 23.9 all-reduce.2
where the time goes:
time: 131 us
  waiting for transfers between devices  49.1 us (37%)
  other arithmetic  20.2 us (15%)
  blocking collectives  19.5 us (15%)
  local copies, waits for them, and re-layouts  18.6 us (14%)
  between operations  14.2 us (11%)
  starting transfers between devices  5.81 us (4%)
  matrix products  3.19 us (2%)
    all_to_all x1, waiting for transfers between devices, body(): lax.all_to_all(summed, 'freq', split_axis=3, concat_axis=1, tiled=True)  26.2 us
    unnamed x2, waiting for transfers between devices  22.9 us
    pmax x1, blocking collectives, body(): whole_peak = lax.pmax(partial_peak, 'freq')  19.5 us
    another operation x1, other arithmetic  7.81 us
    unnamed x9, local copies, waits for them, and re-layouts  6.63 us
    all_to_all x1, starting transfers between devices, body(): lax.all_to_all(summed, 'freq', split_axis=3, concat_axis=1, tiled=True)  5.78 us
    gather x2, local copies, waits for them, and re-layouts, body(): jnp.take(beam_field, flaw_cells, axis=3)  5.75 us
  transfers between devices with their start and end apart: 2, of which 2 were waited for; matrix products, arithmetic and copies ran while one was open for 0% of the time, Pallas kernels for 0%

commit v1 on v0

v1 whole, which is shorter than its diff:
```python
import functools
import math

import jax
import jax.numpy as jnp
from jax import lax
from jax.experimental import pallas as pl
from jax.experimental.pallas import tpu as pltpu
from jax.sharding import PartitionSpec as P

W_DEV = 16
FG = 128
NB = 4
SB = 32
T_CAP = 1024

EDGE = 0.6
STEEP = 3.0
EPS = 1e-05

ROWS = NB * SB
W_STEP = 8
VMEM_BYTES = 48 * 1024 * 1024


def sin_half_turn(turns):
    angle = turns * math.pi
    square = angle * angle
    sine = 1.0 / 6227020800.0
    for factorial in (-39916800.0, 362880.0, -5040.0, 120.0, -6.0, 1.0):
        sine = sine * square + 1.0 / factorial
    cosine = 1.0 / 479001600.0
    for factorial in (-3628800.0, 40320.0, -720.0, 24.0, -2.0, 1.0):
        cosine = cosine * square + 1.0 / factorial
    return sine * angle, cosine


def sincos_turns(turns):
    rest = turns - jnp.floor(turns + 0.5)
    sine, cosine = sin_half_turn(rest)
    return 2.0 * sine * cosine, 1.0 - 2.0 * sine * sine


def dot(left, right, contract):
    return lax.dot_general(
        left, right, (contract, ((), ())), preferred_element_type=jnp.float32
    )


def front_kernel(
    freq_total,
    cells_ref,
    blocks_ref,
    own_channel_ref,
    other_channel_ref,
    delay_ref,
    own_ref,
    other_ref,
    size_ref,
    slope_ref,
    out_ref,
    cos_ref,
    sin_ref,
    step_cos_ref,
    step_sin_ref,
    pick_ref,
    size_col_ref,
    turn_col_ref,
    rows_ref,
):
    step = pl.program_id(0)
    group = lax.axis_index("elem")
    first_freq = lax.axis_index("freq") * W_DEV
    sites = delay_ref.shape[0]

    @pl.when(step == 0)
    def _():
        lane = lax.broadcasted_iota(jnp.int32, (1, ROWS), 1)
        position = lane & (SB - 1)
        for j in range(NB):
            position = position + jnp.where(
                (lane >> 5) == j, blocks_ref[group * NB + j] * SB, 0
            )
        scan_sel = (
            lax.broadcasted_iota(jnp.int32, (delay_ref.shape[1], ROWS), 0) == position
        ).astype(jnp.bfloat16)
        channel_iota = lax.broadcasted_iota(jnp.int32, (delay_ref.shape[0], FG), 0)
        channel_sel = jnp.concatenate(
            [
                (channel_iota == own_channel_ref[...]).astype(jnp.float32),
                (channel_iota == other_channel_ref[...]).astype(jnp.float32),
            ],
            axis=1,
        ).T.astype(jnp.bfloat16)
        rest = delay_ref[...]
        delays = None
        for _piece in range(3):
            piece = rest.astype(jnp.bfloat16)
            rest = rest - piece.astype(jnp.float32)
            moved = dot(piece, scan_sel, ((1,), (0,))).astype(jnp.bfloat16)
            moved = dot(channel_sel, moved, ((1,), (0,)))
            delays = moved if delays is None else delays + moved
        turns = delays * (0.5 / freq_total)
        sine, cosine = sincos_turns(turns)
        step_cos_ref[...] = cosine
        step_sin_ref[...] = sine
        sine, cosine = sincos_turns(turns * first_freq.astype(jnp.float32))
        cos_ref[...] = cosine
        sin_ref[...] = sine
        cells = jnp.where(group == 0, cells_ref[:, :FG], cells_ref[:, FG:])
        cell_sel = lax.broadcasted_iota(jnp.int32, (sites, FG), 0) == cells
        pick_ref[...] = cell_sel.astype(jnp.float32).T.astype(jnp.bfloat16)
        diagonal = lax.broadcasted_iota(
            jnp.int32, (FG, FG), 0
        ) == lax.broadcasted_iota(jnp.int32, (FG, FG), 1)
        size = size_ref[pl.ds(group, 1), :]
        slope = slope_ref[pl.ds(group, 1), :]
        turn = size * slope * (1.0 / freq_total)
        size_col = jnp.sum(jnp.where(diagonal, size, 0.0), axis=1, keepdims=True)
        turn_col = jnp.sum(jnp.where(diagonal, turn, 0.0), axis=1, keepdims=True)
        size_col_ref[...] = jnp.broadcast_to(size_col, (FG, FG))
        turn_col_ref[...] = jnp.broadcast_to(turn_col, (FG, FG))

    freq = first_freq + step * W_STEP + lax.broadcasted_iota(jnp.int32, (FG, FG), 1)
    sine, cosine = sincos_turns(turn_col_ref[...] * freq.astype(jnp.float32))
    k_real = size_col_ref[...] * (1.0 + EDGE) * cosine
    k_imag = size_col_ref[...] * (EDGE - 1.0) * sine
    pick = pick_ref[...]
    cosine = cos_ref[...]
    sine = sin_ref[...]
    step_cos = step_cos_ref[...]
    step_sin = step_sin_ref[...]
    for w in range(W_STEP):
        fields = jnp.concatenate(
            [
                dot(pick, ref[w].reshape(2 * FG, sites), ((1,), (1,))).astype(jnp.bfloat16)
                for ref in (own_ref, other_ref)
            ],
            axis=1,
        )
        c = cosine.astype(jnp.bfloat16)
        s = sine.astype(jnp.bfloat16)
        both = jnp.concatenate([c, -s], axis=1)
        turned = jnp.concatenate([s, c], axis=1)
        law = jnp.concatenate([both[:FG], turned[:FG], both[FG:], turned[FG:]], axis=0)
        product = dot(fields, law, ((1,), (0,)))
        real_part = product[:, :ROWS]
        imag_part = product[:, ROWS:]
        kr = k_real[:, w : w + 1]
        ki = k_imag[:, w : w + 1]
        rows_ref[pl.ds(2 * w, FG, stride=2 * W_STEP), :] = kr * real_part - ki * imag_part
        rows_ref[pl.ds(2 * w + 1, FG, stride=2 * W_STEP), :] = (
            kr * imag_part + ki * real_part
        )
        cosine, sine = (
            cosine * step_cos - sine * step_sin,
            sine * step_cos + cosine * step_sin,
        )
    cos_ref[...] = cosine
    sin_ref[...] = sine
    out_ref[...] = rows_ref[...].reshape(FG, 2 * W_STEP, ROWS).astype(jnp.bfloat16)


def front(
    flaw_cells,
    flaw_blocks,
    own_channel,
    other_channel,
    focal_delay,
    own_field,
    other_field,
    flaw_size,
    flaw_slope,
    freq_total,
):
    def whole(array):
        return pl.BlockSpec(array.shape, lambda i: (0,) * array.ndim)

    small = [
        flaw_cells.reshape(1, -1),
        flaw_blocks,
        own_channel.reshape(1, -1),
        other_channel.reshape(1, -1),
        focal_delay,
    ]
    field_spec = pl.BlockSpec((W_STEP, *own_field.shape[1:]), lambda i: (i, 0, 0, 0))
    elements = 2 * own_channel.shape[0]
    in_specs = [whole(a) for a in small]
    in_specs[1] = pl.BlockSpec(memory_space=pltpu.SMEM)
    in_specs += [field_spec, field_spec, whole(flaw_size), whole(flaw_slope)]
    return pl.pallas_call(
        functools.partial(front_kernel, freq_total),
        grid=(W_DEV // W_STEP,),
        in_specs=in_specs,
        out_specs=pl.BlockSpec((FG, 2 * W_STEP, ROWS), lambda i: (0, i, 0)),
        out_shape=jax.ShapeDtypeStruct((FG, 2 * W_DEV, ROWS), jnp.bfloat16),
        scratch_shapes=[pltpu.VMEM((elements, ROWS), jnp.float32)] * 4
        + [
            pltpu.VMEM((FG, focal_delay.shape[0]), jnp.bfloat16),
            pltpu.VMEM((FG, FG), jnp.float32),
            pltpu.VMEM((FG, FG), jnp.float32),
            pltpu.VMEM((FG * 2 * W_STEP, ROWS), jnp.float32),
        ],
        compiler_params=pltpu.CompilerParams(vmem_limit_bytes=VMEM_BYTES),
        name="front",
    )(*small, own_field, other_field, flaw_size, flaw_slope)


def table_kernel(freq_total, high_ref, low_ref):
    _, height, depth = high_ref.shape
    time_block = height // 2
    row = lax.broadcasted_iota(jnp.int32, (height, depth), 0)
    column = lax.broadcasted_iota(jnp.int32, (height, depth), 1)
    out_imag = (row >= time_block).astype(jnp.int32)
    time = pl.program_id(0) * time_block + row - out_imag * time_block
    steps = (column >> 1) * time + ((column & 1) - out_imag) * (freq_total // 2)
    steps = (steps + 2 * freq_total) & (2 * freq_total - 1)
    _, value = sincos_turns(steps.astype(jnp.float32) * (0.5 / freq_total))
    high = value.astype(jnp.bfloat16)
    high_ref[0] = high
    low_ref[0] = (value - high.astype(jnp.float32)).astype(jnp.bfloat16)


def table(freq_total, sample_count, time_block):
    blocks = sample_count // time_block
    shape = (blocks, 2 * time_block, 2 * freq_total)
    spec = pl.BlockSpec((1, *shape[1:]), lambda i: (i, 0, 0))
    return pl.pallas_call(
        functools.partial(table_kernel, freq_total),
        grid=(blocks,),
        out_specs=[spec, spec],
        out_shape=[jax.ShapeDtypeStruct(shape, jnp.bfloat16)] * 2,
        compiler_params=pltpu.CompilerParams(vmem_limit_bytes=VMEM_BYTES),
        name="table",
    )()


def peak_kernel(freq_total, spectra_ref, high_ref, low_ref, noise_ref, peak_ref, found_ref, best_ref):
    step = pl.program_id(0)
    sources, columns, planes, rows = spectra_ref.shape
    time_block = high_ref.shape[1] // 2

    @pl.when(step == 0)
    def _():
        best_ref[...] = jnp.zeros_like(best_ref)

    high = high_ref[0]
    low = low_ref[0]
    width = min(2, columns)
    for first in range(0, columns, width):
        spectra = jnp.concatenate(
            [
                spectra_ref[:, first + k].reshape(sources * planes, rows)
                for k in range(width)
            ],
            axis=1,
        )
        signal = dot(high, spectra, ((1,), (0,))) + dot(low, spectra, ((1,), (0,)))
        real_part = signal[:time_block]
        imag_part = signal[time_block:]
        power = jnp.max(real_part * real_part + imag_part * imag_part, axis=0, keepdims=True)
        for k in range(width):
            row = pl.ds(first + k, 1)
            best_ref[row, :] = jnp.maximum(
                best_ref[row, :], power[:, k * rows : (k + 1) * rows]
            )

    @pl.when(step == pl.num_programs(0) - 1)
    def _():
        largest = jnp.max(best_ref[...], axis=1, keepdims=True)
        shape = best_ref.shape
        diagonal = lax.broadcasted_iota(jnp.int32, shape, 0) == lax.broadcasted_iota(
            jnp.int32, shape, 1
        )
        largest = jnp.max(jnp.where(diagonal, largest, 0.0), axis=0, keepdims=True)
        peak = jnp.sqrt(largest[:, :columns]) * (1.0 / math.sqrt(freq_total))
        score = STEEP * (jnp.log(peak + EPS) - jnp.log(noise_ref[...]))
        peak_ref[...] = peak
        found_ref[...] = 1.0 / (1.0 + jnp.exp(-score))


def peaks(spectra, high, low, noise_level, freq_total):
    columns = spectra.shape[1]
    blocks = high.shape[0]
    table_spec = pl.BlockSpec((1, *high.shape[1:]), lambda i: (i, 0, 0))
    out_spec = pl.BlockSpec((1, columns), lambda i: (0, 0))
    return pl.pallas_call(
        functools.partial(peak_kernel, freq_total),
        grid=(blocks,),
        in_specs=[
            pl.BlockSpec(spectra.shape, lambda i: (0, 0, 0, 0)),
            table_spec,
            table_spec,
            out_spec,
        ],
        out_specs=[out_spec, out_spec],
        out_shape=[jax.ShapeDtypeStruct((1, columns), jnp.float32)] * 2,
        scratch_shapes=[pltpu.VMEM((max(8, columns), ROWS), jnp.float32)],
        compiler_params=pltpu.CompilerParams(vmem_limit_bytes=VMEM_BYTES),
        name="peaks",
    )(spectra, high, low, noise_level)


def body(
    flaw_cells,
    flaw_blocks,
    element_channel,
    focal_delay,
    beam_field,
    flaw_size,
    flaw_slope,
    noise_level,
):
    freq_count = lax.axis_size("freq")
    freq_total = W_DEV * freq_count
    sample_count = min(T_CAP, 2 * freq_total)
    swap = [(0, 1), (1, 0)]
    other_channel = lax.ppermute(element_channel, "elem", swap)
    other_field = lax.ppermute(beam_field, "elem", swap)
    spectra = front(
        flaw_cells,
        flaw_blocks,
        element_channel,
        other_channel,
        focal_delay,
        beam_field,
        other_field,
        flaw_size,
        flaw_slope,
        freq_total,
    )
    high, low = table(freq_total, sample_count, 256 if freq_total <= 128 else 128)
    moved = lax.all_to_all(spectra, "freq", split_axis=0, concat_axis=0, tiled=True)
    moved = moved.reshape(freq_count, FG // freq_count, 2 * W_DEV, ROWS)
    return tuple(peaks(moved, high, low, noise_level, freq_total))


def solution(mesh):
    in_specs = (
        P("batch"),
        P("batch"),
        P("elem"),
        P(),
        P("freq", None, "elem", None),
        P("batch", None),
        P("batch", None),
        P(("batch", "elem"), "freq"),
    )
    out_specs = (P(("batch", "elem"), "freq"), P(("batch", "elem"), "freq"))
    return jax.shard_map(body, mesh=mesh, in_specs=in_specs, out_specs=out_specs, check_vma=False)
```

time: 131 us -> 52.7 us (0.40)
  other arithmetic: 20.2 us -> 0 us
  waiting for transfers between devices: 49.1 us -> 29.4 us
  blocking collectives: 19.5 us -> 0 us
  between operations: 14.2 us -> 0.65 us
  local copies, waits for them, and re-layouts: 18.6 us -> 5.89 us
  Pallas kernels: 0 us -> 8.53 us
  matrix products: 3.19 us -> 0 us
  starting transfers between devices: 5.81 us -> 7.9 us
    unnamed x2 -> x0, waiting for transfers between devices: 22.9 us -> none
    pmax x1 -> x0, blocking collectives: 19.5 us -> none  [body(): whole_peak = lax.pmax(partial_peak, 'freq')]
    another operation x5 -> x0, other arithmetic: 9.96 us -> none
    pallas_call x0 -> x3, Pallas kernels: none -> 8.53 us  [the longest x1 6.08 us: front(): pl.pallas_call(functools.partial(front_kernel, freq_total), grid=(W_DEV /...]
    gather x4 -> x0, local copies, waits for them, and re-layouts: 7.84 us -> none  [the longest x2 5.75 us: body(): jnp.take(beam_field, flaw_cells, axis=3)]
    select_n x6 -> x0, other arithmetic: 3.99 us -> none  [the longest x2 2.08 us: body(): jnp.take(focal_delay, element_channel, axis=0)]
    ppermute x0 -> x2, waiting for transfers between devices: none -> 3.92 us  [the longest x1 3.92 us: body(): other_channel = lax.ppermute(element_channel, 'elem', swap)]
    dot_general x5 -> x0, matrix products: 3.19 us -> none  [the longest x1 1.41 us: body(): jnp.einsum('wgre,wegf->gwrf', focal_terms, field_terms, preferred_element...]
  transfers between devices with their start and end apart: 2 -> 3, of which waited for: 2 -> 2; matrix products, arithmetic and copies ran while one was open for 0% -> 0% of each run, Pallas kernels for 0% -> 1%
where the time goes in v1:
time: 52.7 us; the launch traced here: 52.4 us
  waiting for transfers between devices  29.4 us (56%)
  Pallas kernels  8.53 us (16%)
  starting transfers between devices  7.9 us (15%)
  local copies, waits for them, and re-layouts  5.89 us (11%)
  between operations  0.65 us (1%)
    all_to_all x1, waiting for transfers between devices, body(): lax.all_to_all(spectra, 'freq', split_axis=0, concat_axis=0, tiled=True)  25.5 us
    all_to_all x1, starting transfers between devices, body(): lax.all_to_all(spectra, 'freq', split_axis=0, concat_axis=0, tiled=True)  7.3 us
    pallas_call x1, Pallas kernels, front(): pl.pallas_call(functools.partial(front_kernel, freq_total), grid=(W_DEV /...  6.08 us
    unnamed x16, local copies, waits for them, and re-layouts  5.89 us
    ppermute x1, waiting for transfers between devices, body(): other_channel = lax.ppermute(element_channel, 'elem', swap)  3.92 us
    pallas_call x1, Pallas kernels, peaks(): pl.pallas_call(functools.partial(peak_kernel, freq_total), grid=(blocks,)...  1.91 us
  transfers between devices with their start and end apart: 3, of which 2 were waited for; matrix products, arithmetic and copies ran while one was open for 0% of the time, Pallas kernels for 1%

profile of v1, /device:TPU:0, one launch (start us, length us, event | category | flops | bytes accessed | tf_op | source)
XLA Modules:
  0.0 52.4 jit_solution(3802549605920771971)
XLA Ops:
  0.6 0.5 collective-permute-start.1
  1.1 0.1 collective-permute-start
  1.2 3.9 %collective-permute-done = s32[128]{0:T(128)S(1)} collective-permute-done((s32[128]{0:T(128)}, s32[128]{0:T(128)S(1)}, u32[]{:S(2)}, u32[]{:S(2)}) %collective-permute-start) | collective-permute-done | bytes 544 | tf_op jit(solution)/shard_map/ppermute | solution.py:318
  5.1 0.0 collective-permute-done.1.other_ref
  5.2 0.0 copy-start
  5.2 1.6 %copy-done = bf16[16,2,128,256]{3,2,1,0:T(8,128)(2,1)S(1)} copy-done((bf16[16,2,128,256]{3,2,1,0:T(8,128)(2,1)S(1)}, bf16[16,2,128,256]{3,2,1,0:T(8,128)(2,1)}, u32[]{:S(2)}) %copy-start) | copy-done | bytes 2097176
  6.7 0.0 copy-start.1
  6.7 0.9 %copy-done.1 = f32[256,256]{1,0:T(8,128)S(1)} copy-done((f32[256,256]{1,0:T(8,128)S(1)}, f32[256,256]{1,0:T(8,128)}, u32[]{:S(2)}) %copy-start.1) | copy-done | bytes 262168
  7.7 0.0 copy-start.2
  7.7 0.7 %copy-done.2 = s32[256]{0:T(256)S(1)} copy-done((s32[256]{0:T(256)S(1)}, s32[256]{0:T(256)}, u32[]{:S(2)}) %copy-start.2) | copy-done | bytes 1048
  8.4 0.0 copy-start.3
  8.4 0.7 %copy-done.3 = f32[2,128]{1,0:T(2,128)S(1)} copy-done((f32[2,128]{1,0:T(2,128)S(1)}, f32[2,128]{1,0:T(2,128)}, u32[]{:S(2)}) %copy-start.3) | copy-done | bytes 1048
  9.1 0.0 copy-start.4
  9.1 0.7 %copy-done.4 = f32[2,128]{1,0:T(2,128)S(1)} copy-done((f32[2,128]{1,0:T(2,128)S(1)}, f32[2,128]{1,0:T(2,128)}, u32[]{:S(2)}) %copy-start.4) | copy-done | bytes 1048
  9.7 0.0 copy-start.5
  9.7 0.7 %copy-done.5 = s32[8]{0:T(128)S(1)} copy-done((s32[8]{0:T(128)S(1)}, s32[8]{0:T(128)}, u32[]{:S(2)}) %copy-start.5) | copy-done | bytes 56
  10.4 0.0 copy-start.6
  10.4 0.7 %copy-done.6 = s32[128]{0:T(128)S(1)} copy-done((s32[128]{0:T(128)S(1)}, s32[128]{0:T(128)}, u32[]{:S(2)}) %copy-start.6) | copy-done | bytes 536
  11.0 6.1 %front.1 = bf16[128,32,128]{2,1,0:T(8,128)(2,1)} custom-call(s32[1,256]{1,0:T(1,128)S(1)} %bitcast.5, s32[8]{0:T(128)S(1)} %copy-done.5, s32[1,128]{1,0:T(1,128)S(1)} %bitcast.6, s32[1,128]{1,0:T(1,128)S(1)} %bitcast.7, f32[256,256]{1,0:T(8,128)S(1)} %copy-done.1, bf16[16,2,128,256]{3,2,1,0:T(8,128)(2,1)S(1)} %copy-done, ...), custom_call_target="tpu_custom_call" | custom-call | tf_op jit(solution)/shard_map/front/pallas_call | solution.py:191
  17.1 0.0 copy-start.7
  17.1 7.3 %all-to-all-start = ((bf16[128,32,128]{2,1,0:T(8,128)(2,1)}), bf16[128,32,128]{2,1,0:T(8,128)(2,1)S(1)}, u32[]{:S(2)}, u32[]{:S(2)}) async-start(bf16[128,32,128]{2,1,0:T(8,128)(2,1)} %front.1), calls=%async_computation | async-start | bytes 2097152 | tf_op jit(solution)/shard_map/all_to_all | solution.py:333
  24.4 0.5 %table.1 = (bf16[1,512,256]{2,1,0:T(8,128)(2,1)S(1)}, bf16[1,512,256]{2,1,0:T(8,128)(2,1)S(1)}) custom-call(), custom_call_target="tpu_custom_call" | custom-call | tf_op jit(solution)/shard_map/table/pallas_call | solution.py:228
  25.0 25.5 %all-to-all-done = bf16[128,32,128]{2,1,0:T(8,128)(2,1)S(1)} async-done(((bf16[128,32,128]{2,1,0:T(8,128)(2,1)}), bf16[128,32,128]{2,1,0:T(8,128)(2,1)S(1)}, u32[]{:S(2)}, u32[]{:S(2)}) %all-to-all-start) | async-done | bytes 1048608 | tf_op jit(solution)/shard_map/all_to_all | solution.py:333
  50.5 0.0 copy-done.7
  50.5 1.9 %peaks.1 = (f32[1,16]{1,0:T(1,128)}, f32[1,16]{1,0:T(1,128)}) custom-call(bf16[8,16,32,128]{3,2,1,0:T(8,128)(2,1)S(1)} %bitcast.4, bf16[1,512,256]{2,1,0:T(8,128)(2,1)S(1)} %get-tuple-element.4.high_ref, bf16[1,512,256]{2,1,0:T(8,128)(2,1)S(1)} %get-tuple-element.5.low_ref, f32[1,16]{1,0:T(1,128)S(1)} %copy-done.7), custom_call_target="tpu_custom_call" | custom-call | tf_op jit(solution)/shard_map/peaks/pallas_call | solution.py:287
Async XLA Ops:
  0.6 4.5 %collective-permute-start.1 = (bf16[16,2,128,256]{3,2,1,0:T(8,128)(2,1)}, bf16[16,2,128,256]{3,2,1,0:T(8,128)(2,1)S(1)}, u32[]{:S(2)}, u32[]{:S(2)}) collective-permute-start(bf16[16,2,128,256]{3,2,1,0:T(8,128)(2,1)} %own_ref.1), channel_id=1, source_target_pairs={{0,1},{1,0},{2,3},{3,2},{4,5},{5,4},{6,7},{7,6},{8,9},{9,8},{10,11... | collective-permute-start | bytes 6291464 | tf_op jit(solution)/shard_map/ppermute | solution.py:319
  1.1 4.0 %collective-permute-start = (s32[128]{0:T(128)}, s32[128]{0:T(128)S(1)}, u32[]{:S(2)}, u32[]{:S(2)}) collective-permute-start(s32[128]{0:T(128)} %param.10), channel_id=1, source_target_pairs={{0,1},{1,0},{2,3},{3,2},{4,5},{5,4},{6,7},{7,6},{8,9},{9,8},{10,11... | collective-permute-start | bytes 1544 | tf_op jit(solution)/shard_map/ppermute | solution.py:318
  5.2 1.6 %copy-start = (bf16[16,2,128,256]{3,2,1,0:T(8,128)(2,1)S(1)}, bf16[16,2,128,256]{3,2,1,0:T(8,128)(2,1)}, u32[]{:S(2)}) copy-start(bf16[16,2,128,256]{3,2,1,0:T(8,128)(2,1)} %own_ref.1) | copy-start | bytes 6291460
  6.7 0.9 %copy-start.1 = (f32[256,256]{1,0:T(8,128)S(1)}, f32[256,256]{1,0:T(8,128)}, u32[]{:S(2)}) copy-start(f32[256,256]{1,0:T(8,128)} %delay_ref.1) | copy-start | bytes 786436
  7.7 0.7 %copy-start.2 = (s32[256]{0:T(256)S(1)}, s32[256]{0:T(256)}, u32[]{:S(2)}) copy-start(s32[256]{0:T(256)} %param.8) | copy-start | bytes 3076
  8.4 0.7 %copy-start.3 = (f32[2,128]{1,0:T(2,128)S(1)}, f32[2,128]{1,0:T(2,128)}, u32[]{:S(2)}) copy-start(f32[2,128]{1,0:T(2,128)} %size_ref.1) | copy-start | bytes 3076
  9.1 0.7 %copy-start.4 = (f32[2,128]{1,0:T(2,128)S(1)}, f32[2,128]{1,0:T(2,128)}, u32[]{:S(2)}) copy-start(f32[2,128]{1,0:T(2,128)} %slope_ref.1) | copy-start | bytes 3076
  9.7 0.7 %copy-start.5 = (s32[8]{0:T(128)S(1)}, s32[8]{0:T(128)}, u32[]{:S(2)}) copy-start(s32[8]{0:T(128)} %blocks_ref.1) | copy-start | bytes 100
  10.4 0.7 %copy-start.6 = (s32[128]{0:T(128)S(1)}, s32[128]{0:T(128)}, u32[]{:S(2)}) copy-start(s32[128]{0:T(128)} %param.10) | copy-start | bytes 1540
  17.1 33.4 %copy-start.7 = (f32[1,16]{1,0:T(1,128)S(1)}, f32[1,16]{1,0:T(1,128)}, u32[]{:S(2)}) copy-start(f32[1,16]{1,0:T(1,128)} %noise_ref.1) | copy-start | bytes 196
  17.1 33.4 %all-to-all-start = ((bf16[128,32,128]{2,1,0:T(8,128)(2,1)}), bf16[128,32,128]{2,1,0:T(8,128)(2,1)S(1)}, u32[]{:S(2)}, u32[]{:S(2)}) async-start(bf16[128,32,128]{2,1,0:T(8,128)(2,1)} %front.1), calls=%async_computation | async-start | bytes 2097152 | tf_op jit(solution)/shard_map/all_to_all | solution.py:333

commit v2 on v1

v2 whole, which is shorter than its diff:
```python
import functools
import math

import jax
import jax.numpy as jnp
from jax import lax
from jax.experimental import pallas as pl
from jax.experimental.pallas import tpu as pltpu
from jax.sharding import PartitionSpec as P

W_DEV = 16
FG = 128
NB = 4
SB = 32
T_CAP = 1024

EDGE = 0.6
STEEP = 3.0
EPS = 1e-05

ROWS = NB * SB
W_STEP = 8
MOST_SLOTS = 8
VMEM_BYTES = 48 * 1024 * 1024


def sin_half_turn(turns):
    angle = turns * math.pi
    square = angle * angle
    sine = 1.0 / 6227020800.0
    for factorial in (-39916800.0, 362880.0, -5040.0, 120.0, -6.0, 1.0):
        sine = sine * square + 1.0 / factorial
    cosine = 1.0 / 479001600.0
    for factorial in (-3628800.0, 40320.0, -720.0, 24.0, -2.0, 1.0):
        cosine = cosine * square + 1.0 / factorial
    return sine * angle, cosine


def sincos_turns(turns):
    rest = turns - jnp.floor(turns + 0.5)
    sine, cosine = sin_half_turn(rest)
    return 2.0 * sine * cosine, 1.0 - 2.0 * sine * sine


def dot(left, right, contract):
    return lax.dot_general(
        left, right, (contract, ((), ())), preferred_element_type=jnp.float32
    )


def slot_order(size, slots):
    row = lax.broadcasted_iota(jnp.int32, (FG, FG), 0)
    column = lax.broadcasted_iota(jnp.int32, (FG, FG), 1)
    if slots > 1:
        row = row ^ (lax.axis_index("freq") * size)
    return row == column


def partial_kernel(freq_total, slots, first_step, *refs):
    if first_step == 0:
        (
            cells_ref,
            size_ref,
            slope_ref,
            field_hbm,
            blocks_ref,
            channel_ref,
            delay_hbm,
            other_ref,
            own_ref,
            next_cos_ref,
            next_sin_ref,
            step_cos_ref,
            step_sin_ref,
            field_ref,
            field_sem,
            delay_ref,
            delay_sem,
            picked_ref,
            law_ref,
            rows_ref,
        ) = refs
    else:
        (
            cells_ref,
            size_ref,
            slope_ref,
            field_hbm,
            cos_ref,
            sin_ref,
            step_cos_ref,
            step_sin_ref,
            other_ref,
            own_ref,
            field_ref,
            field_sem,
            picked_ref,
            law_ref,
            rows_ref,
        ) = refs
    field_copy = pltpu.make_async_copy(
        field_hbm.at[pl.ds(first_step * W_STEP, W_STEP)], field_ref, field_sem
    )
    field_copy.start()
    if first_step == 0:
        delay_copy = pltpu.make_async_copy(delay_hbm, delay_ref, delay_sem)
        delay_copy.start()
    group = lax.axis_index("elem")
    other = 1 - group
    first_freq = lax.axis_index("freq") * W_DEV
    elements, sites = field_ref.shape[2:]

    order = slot_order(FG // slots, slots)
    order_sel = order.astype(jnp.bfloat16)
    picks, sizes, turns = [], [], []
    for which in (other, group):
        cells = jnp.where(which == 0, cells_ref[:, :FG], cells_ref[:, FG:])
        cell_sel = lax.broadcasted_iota(jnp.int32, (sites, FG), 0) == cells
        picks.append(dot(order_sel, cell_sel.astype(jnp.bfloat16), ((1,), (1,))))
        size = size_ref[pl.ds(which, 1), :]
        turn = size * slope_ref[pl.ds(which, 1), :] * (1.0 / freq_total)
        sizes.append(jnp.sum(jnp.where(order, size, 0.0), axis=1, keepdims=True))
        turns.append(jnp.sum(jnp.where(order, turn, 0.0), axis=1, keepdims=True))
    pick = jnp.concatenate(picks, axis=0).astype(jnp.bfloat16)
    size = jnp.concatenate(sizes, axis=0)
    turn = jnp.concatenate(turns, axis=0)
    freq = (
        first_freq
        + first_step * W_STEP
        + lax.broadcasted_iota(jnp.int32, (2 * FG, FG), 1)
    )
    sine, cosine = sincos_turns(turn * freq.astype(jnp.float32))
    k_real = size * (1.0 + EDGE) * cosine
    k_imag = size * (EDGE - 1.0) * sine

    if first_step == 0:
        lane = lax.broadcasted_iota(jnp.int32, (1, 2 * ROWS), 1)
        position = lane & (SB - 1)
        for j in range(2 * NB):
            block = blocks_ref[(other if j < NB else group) * NB + j % NB]
            position = position + jnp.where((lane >> 5) == j, block * SB, 0)
        scan_sel = (
            lax.broadcasted_iota(jnp.int32, (delay_ref.shape[1], 2 * ROWS), 0) == position
        ).astype(jnp.bfloat16)
        channel_sel = (
            (
                lax.broadcasted_iota(jnp.int32, (delay_ref.shape[0], elements), 0)
                == channel_ref[...]
            )
            .astype(jnp.float32)
            .T.astype(jnp.bfloat16)
        )
        delay_copy.wait()
        rest = delay_ref[...]
        delays = None
        for _piece in range(3):
            piece = rest.astype(jnp.bfloat16)
            rest = rest - piece.astype(jnp.float32)
            moved = dot(channel_sel, piece, ((1,), (0,))).astype(jnp.bfloat16)
            moved = dot(moved, scan_sel, ((1,), (0,)))
            delays = moved if delays is None else delays + moved
        phase = delays * (0.5 / freq_total)
        step_sin, step_cos = sincos_turns(phase)
        step_cos_ref[...] = step_cos
        step_sin_ref[...] = step_sin
        sine, cosine = sincos_turns(phase * first_freq.astype(jnp.float32))
    else:
        cosine = cos_ref[...]
        sine = sin_ref[...]
        step_cos = step_cos_ref[...]
        step_sin = step_sin_ref[...]

    for w in range(W_STEP):
        c = cosine.astype(jnp.bfloat16)
        s = sine.astype(jnp.bfloat16)
        for k in range(2):
            columns = slice(k * ROWS, (k + 1) * ROWS)
            law_ref[w, k, :elements, :ROWS] = c[:, columns]
            law_ref[w, k, :elements, ROWS:] = -s[:, columns]
            law_ref[w, k, elements:, :ROWS] = s[:, columns]
            law_ref[w, k, elements:, ROWS:] = c[:, columns]
        if w < W_STEP - 1 or first_step == 0:
            cosine, sine = (
                cosine * step_cos - sine * step_sin,
                sine * step_cos + cosine * step_sin,
            )
    if first_step == 0:
        next_cos_ref[...] = cosine
        next_sin_ref[...] = sine

    field_copy.wait()
    for w in range(W_STEP):
        picked_ref[w] = dot(
            pick, field_ref[w].reshape(2 * elements, sites), ((1,), (1,))
        ).astype(jnp.bfloat16)
    for k, out_ref in enumerate((other_ref, own_ref)):
        rows = slice(k * FG, (k + 1) * FG)
        for w in range(W_STEP):
            product = dot(picked_ref[w, rows, :], law_ref[w, k], ((1,), (0,)))
            real_part = product[:, :ROWS]
            imag_part = product[:, ROWS:]
            kr = k_real[rows, w : w + 1]
            ki = k_imag[rows, w : w + 1]
            rows_ref[k, pl.ds(2 * w, FG, stride=2 * W_STEP), :] = (
                kr * real_part - ki * imag_part
            )
            rows_ref[k, pl.ds(2 * w + 1, FG, stride=2 * W_STEP), :] = (
                kr * imag_part + ki * real_part
            )
        out_ref[...] = (
            rows_ref[k].reshape(FG, 2 * W_STEP, ROWS).astype(jnp.bfloat16)
        )


def partials(small, field, extra, freq_total, slots, first_step):
    elements, sites = field.shape[2:]
    vmem = pl.BlockSpec(memory_space=pltpu.VMEM)
    hbm = pl.BlockSpec(memory_space=pltpu.HBM)
    smem = pl.BlockSpec(memory_space=pltpu.SMEM)
    out_shape = [jax.ShapeDtypeStruct((FG, 2 * W_STEP, ROWS), jnp.bfloat16)] * 2
    scratch = [
        pltpu.VMEM((W_STEP, 2, elements, sites), jnp.bfloat16),
        pltpu.SemaphoreType.DMA,
    ]
    if first_step == 0:
        extra_specs = [smem, vmem, hbm]
        out_shape += [jax.ShapeDtypeStruct((elements, 2 * ROWS), jnp.float32)] * 4
        scratch += [pltpu.VMEM(extra[2].shape, jnp.float32), pltpu.SemaphoreType.DMA]
    else:
        extra_specs = [vmem] * 4
    scratch += [
        pltpu.VMEM((W_STEP, 2 * FG, 2 * elements), jnp.bfloat16),
        pltpu.VMEM((W_STEP, 2, 2 * elements, 2 * ROWS), jnp.bfloat16),
        pltpu.VMEM((2, FG * 2 * W_STEP, ROWS), jnp.float32),
    ]
    return pl.pallas_call(
        functools.partial(partial_kernel, freq_total, slots, first_step),
        in_specs=[vmem] * 3 + [hbm] + extra_specs,
        out_specs=[vmem] * len(out_shape),
        out_shape=out_shape,
        scratch_shapes=scratch,
        compiler_params=pltpu.CompilerParams(vmem_limit_bytes=VMEM_BYTES),
        cost_estimate=pl.CostEstimate(
            flops=2 * W_STEP * 2 * 256**3, bytes_accessed=3 << 20, transcendentals=0
        ),
        name=f"partials_{first_step}",
    )(*small, field, *extra)


def add_kernel(own_ref, moved_ref, *out_refs):
    size = out_refs[0].shape[0]
    for slot, out_ref in enumerate(out_refs):
        rows = pl.ds(slot * size, size)
        out_ref[...] = (
            own_ref[rows].astype(jnp.float32) + moved_ref[rows].astype(jnp.float32)
        ).astype(jnp.bfloat16)


def add(own, moved, slots):
    vmem = pl.BlockSpec(memory_space=pltpu.VMEM)
    shape = jax.ShapeDtypeStruct((FG // slots, *own.shape[1:]), jnp.bfloat16)
    return pl.pallas_call(
        add_kernel,
        in_specs=[vmem, vmem],
        out_specs=[vmem] * slots,
        out_shape=[shape] * slots,
        compiler_params=pltpu.CompilerParams(vmem_limit_bytes=VMEM_BYTES),
        cost_estimate=pl.CostEstimate(flops=0, bytes_accessed=3 << 19, transcendentals=0),
        name="add_groups",
    )(own, moved)


def table_kernel(freq_total, slots, high_ref, low_ref):
    _, height, depth = high_ref.shape
    time_block = height // 2
    row = lax.broadcasted_iota(jnp.int32, (height, depth), 0)
    column = lax.broadcasted_iota(jnp.int32, (height, depth), 1)
    out_imag = (row >= time_block).astype(jnp.int32)
    time = pl.program_id(0) * time_block + row - out_imag * time_block
    freq = column >> 1
    if slots > 1:
        freq = freq ^ (lax.axis_index("freq") * W_DEV)
    steps = freq * time + ((column & 1) - out_imag) * (freq_total // 2)
    steps = (steps + 2 * freq_total) & (2 * freq_total - 1)
    _, value = sincos_turns(steps.astype(jnp.float32) * (0.5 / freq_total))
    high = value.astype(jnp.bfloat16)
    high_ref[0] = high
    low_ref[0] = (value - high.astype(jnp.float32)).astype(jnp.bfloat16)


def table(freq_total, slots, sample_count, time_block):
    blocks = sample_count // time_block
    shape = (blocks, 2 * time_block, 2 * freq_total)
    spec = pl.BlockSpec((1, *shape[1:]), lambda i: (i, 0, 0))
    return pl.pallas_call(
        functools.partial(table_kernel, freq_total, slots),
        grid=(blocks,),
        out_specs=[spec, spec],
        out_shape=[jax.ShapeDtypeStruct(shape, jnp.bfloat16)] * 2,
        compiler_params=pltpu.CompilerParams(vmem_limit_bytes=VMEM_BYTES),
        name="table",
    )()


def peak_kernel(freq_total, count, *refs):
    spectra_refs = refs[:count]
    high_ref, low_ref, noise_ref, peak_ref, found_ref, best_ref = refs[count:]
    step = pl.program_id(0)
    columns = peak_ref.shape[1]
    rows = ROWS
    time_block = high_ref.shape[1] // 2

    @pl.when(step == 0)
    def _():
        best_ref[...] = jnp.zeros_like(best_ref)

    high = high_ref[0]
    low = low_ref[0]
    width = min(2, columns)
    for first in range(0, columns, width):
        spectra = jnp.concatenate(
            [
                jnp.concatenate(
                    [ref[:, first + k].reshape(-1, rows) for ref in spectra_refs], axis=0
                )
                for k in range(width)
            ],
            axis=1,
        )
        signal = dot(high, spectra, ((1,), (0,))) + dot(low, spectra, ((1,), (0,)))
        real_part = signal[:time_block]
        imag_part = signal[time_block:]
        power = jnp.max(real_part * real_part + imag_part * imag_part, axis=0, keepdims=True)
        for k in range(width):
            row = pl.ds(first + k, 1)
            best_ref[row, :] = jnp.maximum(
                best_ref[row, :], power[:, k * rows : (k + 1) * rows]
            )

    @pl.when(step == pl.num_programs(0) - 1)
    def _():
        largest = jnp.max(best_ref[...], axis=1, keepdims=True)
        shape = best_ref.shape
        diagonal = lax.broadcasted_iota(jnp.int32, shape, 0) == lax.broadcasted_iota(
            jnp.int32, shape, 1
        )
        largest = jnp.max(jnp.where(diagonal, largest, 0.0), axis=0, keepdims=True)
        peak = jnp.sqrt(largest[:, :columns]) * (1.0 / math.sqrt(freq_total))
        score = STEEP * (jnp.log(peak + EPS) - jnp.log(noise_ref[...]))
        peak_ref[...] = peak
        found_ref[...] = 1.0 / (1.0 + jnp.exp(-score))


def peaks(spectra, high, low, noise_level, freq_total):
    columns = noise_level.shape[1]
    blocks = high.shape[0]
    table_spec = pl.BlockSpec((1, *high.shape[1:]), lambda i: (i, 0, 0))
    out_spec = pl.BlockSpec((1, columns), lambda i: (0, 0))
    return pl.pallas_call(
        functools.partial(peak_kernel, freq_total, len(spectra)),
        grid=(blocks,),
        in_specs=[pl.BlockSpec(a.shape, lambda i: (0, 0, 0, 0)) for a in spectra]
        + [table_spec, table_spec, out_spec],
        out_specs=[out_spec, out_spec],
        out_shape=[jax.ShapeDtypeStruct((1, columns), jnp.float32)] * 2,
        scratch_shapes=[pltpu.VMEM((max(8, columns), ROWS), jnp.float32)],
        compiler_params=pltpu.CompilerParams(vmem_limit_bytes=VMEM_BYTES),
        name="peaks",
    )(*spectra, high, low, noise_level)


def body(
    flaw_cells,
    flaw_blocks,
    element_channel,
    focal_delay,
    beam_field,
    flaw_size,
    flaw_slope,
    noise_level,
):
    freq_count = lax.axis_size("freq")
    freq_total = W_DEV * freq_count
    sample_count = min(T_CAP, 2 * freq_total)
    swap = [(0, 1), (1, 0)]
    slots = freq_count if freq_count <= MOST_SLOTS else 1
    small = (flaw_cells.reshape(1, -1), flaw_size, flaw_slope)
    extra = (flaw_blocks, element_channel.reshape(1, -1), focal_delay)
    chunks = []
    for first_step in range(W_DEV // W_STEP):
        other, own, *state = partials(small, beam_field, extra, freq_total, slots, first_step)
        extra = state if state else extra
        chunks.append(add(own, lax.ppermute(other, "elem", swap), slots))
    high, low = table(freq_total, slots, sample_count, 256 if freq_total <= 128 else 128)
    if slots > 1:
        spectra = []
        for slot in range(slots):
            pairs = [(a, a ^ slot) for a in range(slots)]
            for chunk in chunks:
                moved = lax.ppermute(chunk[slot], "freq", pairs) if slot else chunk[slot]
                spectra.append(moved[None])
    else:
        moved = lax.all_to_all(
            jnp.concatenate([chunk[0] for chunk in chunks], axis=1),
            "freq",
            split_axis=0,
            concat_axis=0,
            tiled=True,
        )
        spectra = [moved.reshape(freq_count, FG // freq_count, 2 * W_DEV, ROWS)]
    return tuple(peaks(spectra, high, low, noise_level, freq_total))


def solution(mesh):
    in_specs = (
        P("batch"),
        P("batch"),
        P("elem"),
        P(),
        P("freq", None, "elem", None),
        P("batch", None),
        P("batch", None),
        P(("batch", "elem"), "freq"),
    )
    out_specs = (P(("batch", "elem"), "freq"), P(("batch", "elem"), "freq"))
    return jax.shard_map(body, mesh=mesh, in_specs=in_specs, out_specs=out_specs, check_vma=False)
```

time: 52.7 us -> 49.3 us (0.935)
  waiting for transfers between devices: 29.4 us -> 4.67 us
  starting transfers between devices: 7.9 us -> 29.2 us
    ppermute x2 -> x16, starting transfers between devices: 0.6 us -> 29.2 us  [the longest x14 28.6 us: body(): moved = lax.ppermute(chunk[slot], 'freq', pairs) if slot else chunk[slot]]
    all_to_all x1 -> x0, waiting for transfers between devices: 25.5 us -> none  [body(): lax.all_to_all(spectra, 'freq', split_axis=0, concat_axis=0, tiled=True)]
    all_to_all x1 -> x0, starting transfers between devices: 7.3 us -> none  [body(): lax.all_to_all(spectra, 'freq', split_axis=0, concat_axis=0, tiled=True)]
    ppermute x2 -> x16, waiting for transfers between devices: 3.92 us -> 4.67 us  [the longest x14 4.67 us: body(): moved = lax.ppermute(chunk[slot], 'freq', pairs) if slot else chunk[slot]]
    pallas_call x3 -> x6, Pallas kernels: 8.53 us -> 8.54 us  [the longest x2 5.82 us: partials(): pl.pallas_call(functools.partial(partial_kernel, freq_total, slots, first...]
  transfers between devices with their start and end apart: 3 -> 16, of which waited for: 2 -> 3; matrix products, arithmetic and copies ran while one was open for 0% -> 0% of each run, Pallas kernels for 1% -> 7%
where the time goes in v2:
time: 49.3 us; the launch traced here: 49 us
  starting transfers between devices  29.2 us (59%)
  Pallas kernels  8.54 us (17%)
  local copies, waits for them, and re-layouts  5.88 us (12%)
  waiting for transfers between devices  4.67 us (9%)
  between operations  0.71 us (1%)
    ppermute x14, starting transfers between devices, body(): moved = lax.ppermute(chunk[slot], 'freq', pairs) if slot else chunk[slot]  28.6 us
    unnamed x16, local copies, waits for them, and re-layouts  5.88 us
    pallas_call x2, Pallas kernels, partials(): pl.pallas_call(functools.partial(partial_kernel, freq_total, slots, first...  5.82 us
    ppermute x14, waiting for transfers between devices, body(): moved = lax.ppermute(chunk[slot], 'freq', pairs) if slot else chunk[slot]  4.67 us
    pallas_call x1, Pallas kernels, peaks(): pl.pallas_call(functools.partial(peak_kernel, freq_total, len(spectra)),...  1.92 us
  transfers between devices with their start and end apart: 16, of which 3 were waited for; matrix products, arithmetic and copies ran while one was open for 0% of the time, Pallas kernels for 7%

profile of v2, /device:TPU:0, one launch (start us, length us, event | category | flops | bytes accessed | tf_op | source)
XLA Modules:
  0.0 49.0 jit_solution(11714354358273379185)
XLA Ops:
  0.6 0.0 copy-start
  0.6 1.6 %copy-done = bf16[16,2,128,256]{3,2,1,0:T(8,128)(2,1)S(1)} copy-done((bf16[16,2,128,256]{3,2,1,0:T(8,128)(2,1)S(1)}, bf16[16,2,128,256]{3,2,1,0:T(8,128)(2,1)}, u32[]{:S(2)}) %copy-start) | copy-done | bytes 2097176
  2.2 0.0 copy-start.1
  2.2 0.9 %copy-done.1 = f32[256,256]{1,0:T(8,128)S(1)} copy-done((f32[256,256]{1,0:T(8,128)S(1)}, f32[256,256]{1,0:T(8,128)}, u32[]{:S(2)}) %copy-start.1) | copy-done | bytes 262168
  3.2 0.0 copy-start.2
  3.2 0.7 %copy-done.2 = s32[256]{0:T(256)S(1)} copy-done((s32[256]{0:T(256)S(1)}, s32[256]{0:T(256)}, u32[]{:S(2)}) %copy-start.2) | copy-done | bytes 1048
  3.9 0.0 copy-start.3
  3.9 0.7 %copy-done.3 = f32[2,128]{1,0:T(2,128)S(1)} copy-done((f32[2,128]{1,0:T(2,128)S(1)}, f32[2,128]{1,0:T(2,128)}, u32[]{:S(2)}) %copy-start.3) | copy-done | bytes 1048
  4.5 0.0 copy-start.4
  4.5 0.7 %copy-done.4 = f32[2,128]{1,0:T(2,128)S(1)} copy-done((f32[2,128]{1,0:T(2,128)S(1)}, f32[2,128]{1,0:T(2,128)}, u32[]{:S(2)}) %copy-start.4) | copy-done | bytes 1048
  5.2 0.0 copy-start.5
  5.2 0.7 %copy-done.5 = s32[8]{0:T(128)S(1)} copy-done((s32[8]{0:T(128)S(1)}, s32[8]{0:T(128)}, u32[]{:S(2)}) %copy-start.5) | copy-done | bytes 56
  5.9 0.0 copy-start.6
  5.9 0.7 %copy-done.6 = s32[128]{0:T(128)S(1)} copy-done((s32[128]{0:T(128)S(1)}, s32[128]{0:T(128)}, u32[]{:S(2)}) %copy-start.6) | copy-done | bytes 536
  6.5 3.4 %partials_0.1 = (bf16[128,16,128]{2,1,0:T(8,128)(2,1)S(1)}, bf16[128,16,128]{2,1,0:T(8,128)(2,1)S(1)}, f32[128,256]{1,0:T(8,128)S(1)}, f32[128,256]{1,0:T(8,128)...) custom-call(s32[1,256]{1,0:T(1,128)S(1)} %bitcast.34, f32[2,128]{1,0:T(2,128)S(1)} %copy-done.3, ...), custom_call_target="tpu_custom_call" | custom-call | flops 536870912 | bytes 3145728 | tf_op jit(solution)/shard_map/partials_0/pallas_call | solution.py:236
  9.9 0.5 %collective-permute-start = (bf16[128,16,128]{2,1,0:T(8,128)(2,1)S(1)}, bf16[128,16,128]{2,1,0:T(8,128)(2,1)S(1)}, u32[]{:S(2)}, u32[]{:S(2)}) collective-permute-start(bf16[128,16,128]{2,1,0:T(8,128)(2,1)S(1)} %get-tuple-element.29), channel_id=1, source_target_pairs={{0,1},{1,0},{2,3},{3,2},{4,5},{5,4},{6,7},{7,6},{8,9},{9,8},{10,11... | collective-permute-start | bytes 1572872 | tf_op jit(solution)/shard_map/ppermute | solution.py:393
  10.5 0.0 copy-start.7
  10.5 2.4 %partials_1.1 = (bf16[128,16,128]{2,1,0:T(8,128)(2,1)S(1)}, bf16[128,16,128]{2,1,0:T(8,128)(2,1)S(1)}) custom-call(s32[1,256]{1,0:T(1,128)S(1)} %bitcast.35, f32[2,128]{1,0:T(2,128)S(1)} %copy-done.3, f32[2,128]{1,0:T(2,128)S(1)} %copy-done.4, bf16[16,2,128,256]{3,2,1,0:T(8,128)(2,1)S(1)} %copy-done, f32[128,256]{1,0:T(8,128)S(1)} %get-tuple-element.31.refs_4_, ...), custom_call_target="tpu_custom_call" | custom-call | flops 536870912 | bytes 3145728 | tf_op jit(solution)/shard_map/partials_1/pallas_call | solution.py:236
  12.9 0.1 collective-permute-start.1
  13.0 0.0 collective-permute-done.moved_ref
  13.0 0.1 add_groups.2
  13.1 3.0 %collective-permute-start.2 = (bf16[16,16,128]{2,1,0:T(8,128)(2,1)S(1)}, bf16[16,16,128]{2,1,0:T(8,128)(2,1)S(1)}, u32[]{:S(2)}, u32[]{:S(2)}) collective-permute-start(bf16[16,16,128]{2,1,0:T(8,128)(2,1)S(1)} %get-tuple-element.38), channel_id=1, source_target_pairs={{0,2},{2,0},{4,6},{6,4},{8,10},{10,8},{12,14},{14,12},{1,3},{3,1},... | collective-permute-start | bytes 196616 | tf_op jit(solution)/shard_map/ppermute | solution.py:400
  16.1 0.0 collective-permute-done.1.moved_ref
  16.1 0.1 add_groups.3
  16.3 1.4 %collective-permute-start.3 = (bf16[16,16,128]{2,1,0:T(8,128)(2,1)S(1)}, bf16[16,16,128]{2,1,0:T(8,128)(2,1)S(1)}, u32[]{:S(2)}, u32[]{:S(2)}) collective-permute-start(bf16[16,16,128]{2,1,0:T(8,128)(2,1)S(1)} %get-tuple-element.39), channel_id=1, source_target_pairs={{0,2},{2,0},{4,6},{6,4},{8,10},{10,8},{12,14},{14,12},{1,3},{3,1},... | collective-permute-start | bytes 196616 | tf_op jit(solution)/shard_map/ppermute | solution.py:400
  17.7 1.6 %collective-permute-start.4 = (bf16[16,16,128]{2,1,0:T(8,128)(2,1)S(1)}, bf16[16,16,128]{2,1,0:T(8,128)(2,1)S(1)}, u32[]{:S(2)}, u32[]{:S(2)}) collective-permute-start(bf16[16,16,128]{2,1,0:T(8,128)(2,1)S(1)} %get-tuple-element.40), channel_id=1, source_target_pairs={{0,4},{2,6},{4,0},{6,2},{8,12},{10,14},{12,8},{14,10},{1,5},{3,7},... | collective-permute-start | bytes 196616 | tf_op jit(solution)/shard_map/ppermute | solution.py:400
  19.3 0.4 collective-permute-start.5
  19.7 1.7 %collective-permute-start.6 = (bf16[16,16,128]{2,1,0:T(8,128)(2,1)S(1)}, bf16[16,16,128]{2,1,0:T(8,128)(2,1)S(1)}, u32[]{:S(2)}, u32[]{:S(2)}) collective-permute-start(bf16[16,16,128]{2,1,0:T(8,128)(2,1)S(1)} %get-tuple-element.42), channel_id=1, source_target_pairs={{0,6},{2,4},{4,2},{6,0},{8,14},{10,12},{12,10},{14,8},{1,7},{3,5},... | collective-permute-start | bytes 196616 | tf_op jit(solution)/shard_map/ppermute | solution.py:400
  21.4 0.0 collective-permute-done.2
  21.4 1.2 %collective-permute-start.7 = (bf16[16,16,128]{2,1,0:T(8,128)(2,1)S(1)}, bf16[16,16,128]{2,1,0:T(8,128)(2,1)S(1)}, u32[]{:S(2)}, u32[]{:S(2)}) collective-permute-start(bf16[16,16,128]{2,1,0:T(8,128)(2,1)S(1)} %get-tuple-element.43), channel_id=1, source_target_pairs={{0,6},{2,4},{4,2},{6,0},{8,14},{10,12},{12,10},{14,8},{1,7},{3,5},... | collective-permute-start | bytes 196616 | tf_op jit(solution)/shard_map/ppermute | solution.py:400
  22.7 0.0 collective-permute-done.3
  22.7 2.6 %collective-permute-start.8 = (bf16[16,16,128]{2,1,0:T(8,128)(2,1)S(1)}, bf16[16,16,128]{2,1,0:T(8,128)(2,1)S(1)}, u32[]{:S(2)}, u32[]{:S(2)}) collective-permute-start(bf16[16,16,128]{2,1,0:T(8,128)(2,1)S(1)} %get-tuple-element.44), channel_id=1, source_target_pairs={{0,8},{2,10},{4,12},{6,14},{8,0},{10,2},{12,4},{14,6},{1,9},{3,11}... | collective-permute-start | bytes 196616 | tf_op jit(solution)/shard_map/ppermute | solution.py:400
  25.2 0.0 collective-permute-done.4
  25.3 0.3 collective-permute-start.9
  25.6 0.0 collective-permute-done.5
  25.6 2.7 %collective-permute-start.10 = (bf16[16,16,128]{2,1,0:T(8,128)(2,1)S(1)}, bf16[16,16,128]{2,1,0:T(8,128)(2,1)S(1)}, u32[]{:S(2)}, u32[]{:S(2)}) collective-permute-start(bf16[16,16,128]{2,1,0:T(8,128)(2,1)S(1)} %get-tuple-element.46), channel_id=1, source_target_pairs={{0,10},{2,8},{4,14},{6,12},{8,2},{10,0},{12,6},{14,4},{1,11},{3,9}... | collective-permute-start | bytes 196616 | tf_op jit(solution)/shard_map/ppermute | solution.py:400
  28.3 0.0 collective-permute-done.6
  28.3 1.1 %collective-permute-start.11 = (bf16[16,16,128]{2,1,0:T(8,128)(2,1)S(1)}, bf16[16,16,128]{2,1,0:T(8,128)(2,1)S(1)}, u32[]{:S(2)}, u32[]{:S(2)}) collective-permute-start(bf16[16,16,128]{2,1,0:T(8,128)(2,1)S(1)} %get-tuple-element.47), channel_id=1, source_target_pairs={{0,10},{2,8},{4,14},{6,12},{8,2},{10,0},{12,6},{14,4},{1,11},{3,9}... | collective-permute-start | bytes 196616 | tf_op jit(solution)/shard_map/ppermute | solution.py:400
  29.4 0.0 collective-permute-done.7
  29.4 3.6 %collective-permute-start.12 = (bf16[16,16,128]{2,1,0:T(8,128)(2,1)S(1)}, bf16[16,16,128]{2,1,0:T(8,128)(2,1)S(1)}, u32[]{:S(2)}, u32[]{:S(2)}) collective-permute-start(bf16[16,16,128]{2,1,0:T(8,128)(2,1)S(1)} %get-tuple-element.48), channel_id=1, source_target_pairs={{0,12},{2,14},{4,8},{6,10},{8,4},{10,6},{12,0},{14,2},{1,13},{3,15... | collective-permute-start | bytes 196616 | tf_op jit(solution)/shard_map/ppermute | solution.py:400
  33.0 0.8 %collective-permute-done.8 = bf16[16,16,128]{2,1,0:T(8,128)(2,1)S(1)} collective-permute-done((bf16[16,16,128]{2,1,0:T(8,128)(2,1)S(1)}, bf16[16,16,128]{2,1,0:T(8,128)(2,1)S(1)}, u32[]{:S(2)}, u32[]{:S(2)}) %collective-permute-start.8) | collective-permute-done | bytes 65568 | tf_op jit(solution)/shard_map/ppermute | solution.py:400
  33.8 4.1 %collective-permute-start.13 = (bf16[16,16,128]{2,1,0:T(8,128)(2,1)S(1)}, bf16[16,16,128]{2,1,0:T(8,128)(2,1)S(1)}, u32[]{:S(2)}, u32[]{:S(2)}) collective-permute-start(bf16[16,16,128]{2,1,0:T(8,128)(2,1)S(1)} %get-tuple-element.49), channel_id=1, source_target_pairs={{0,12},{2,14},{4,8},{6,10},{8,4},{10,6},{12,0},{14,2},{1,13},{3,15... | collective-permute-start | bytes 196616 | tf_op jit(solution)/shard_map/ppermute | solution.py:400
  38.0 0.0 collective-permute-done.9
  38.0 2.1 %collective-permute-start.14 = (bf16[16,16,128]{2,1,0:T(8,128)(2,1)S(1)}, bf16[16,16,128]{2,1,0:T(8,128)(2,1)S(1)}, u32[]{:S(2)}, u32[]{:S(2)}) collective-permute-start(bf16[16,16,128]{2,1,0:T(8,128)(2,1)S(1)} %get-tuple-element.50), channel_id=1, source_target_pairs={{0,14},{2,12},{4,10},{6,8},{8,6},{10,4},{12,2},{14,0},{1,15},{3,13... | collective-permute-start | bytes 196616 | tf_op jit(solution)/shard_map/ppermute | solution.py:400
  40.0 0.0 collective-permute-done.10
  40.0 2.6 %collective-permute-start.15 = (bf16[16,16,128]{2,1,0:T(8,128)(2,1)S(1)}, bf16[16,16,128]{2,1,0:T(8,128)(2,1)S(1)}, u32[]{:S(2)}, u32[]{:S(2)}) collective-permute-start(bf16[16,16,128]{2,1,0:T(8,128)(2,1)S(1)} %get-tuple-element.51), channel_id=1, source_target_pairs={{0,14},{2,12},{4,10},{6,8},{8,6},{10,4},{12,2},{14,0},{1,15},{3,13... | collective-permute-start | bytes 196616 | tf_op jit(solution)/shard_map/ppermute | solution.py:400
  42.7 0.5 %table.1 = (bf16[1,512,256]{2,1,0:T(8,128)(2,1)S(1)}, bf16[1,512,256]{2,1,0:T(8,128)(2,1)S(1)}) custom-call(), custom_call_target="tpu_custom_call" | custom-call | tf_op jit(solution)/shard_map/table/pallas_call | solution.py:295
  43.2 0.0 collective-permute-done.11
  43.2 0.0 collective-permute-done.12
  43.3 0.0 collective-permute-done.13
  43.3 1.7 %collective-permute-done.14 = bf16[16,16,128]{2,1,0:T(8,128)(2,1)S(1)} collective-permute-done((bf16[16,16,128]{2,1,0:T(8,128)(2,1)S(1)}, bf16[16,16,128]{2,1,0:T(8,128)(2,1)S(1)}, u32[]{:S(2)}, u32[]{:S(2)}) %collective-permute-start.14) | collective-permute-done | bytes 65568 | tf_op jit(solution)/shard_map/ppermute | solution.py:400
  44.9 2.2 %collective-permute-done.15 = bf16[16,16,128]{2,1,0:T(8,128)(2,1)S(1)} collective-permute-done((bf16[16,16,128]{2,1,0:T(8,128)(2,1)S(1)}, bf16[16,16,128]{2,1,0:T(8,128)(2,1)S(1)}, u32[]{:S(2)}, u32[]{:S(2)}) %collective-permute-start.15) | collective-permute-done | bytes 65568 | tf_op jit(solution)/shard_map/ppermute | solution.py:400
  47.1 0.0 copy-done.7
  47.1 1.9 %peaks.1 = (f32[1,16]{1,0:T(1,128)}, f32[1,16]{1,0:T(1,128)}) custom-call(bf16[1,16,16,128]{3,2,1,0:T(8,128)(2,1)S(1)} %bitcast.18, bf16[1,16,16,128]{3,2,1,0:T(8,128)(2,1)S(1)} %bitcast.20, bf16[1,16,16,128]{3,2,1,0:T(8,128)(2,1)S(1)} %bitcast.19, bf16[1,16,16,128]{3,2,1,0:T(8,128)(2,1)S(1)} %bitcast.21, bf16[1,16,16,128]{3,2,1,0:T(8,128)(2,1)S(1)} %bitcast.22, ...), custom_call_target="tpu_custom_call" | custom-call | tf_op jit(solution)/shard_map/peaks/pallas_call | solution.py:359
Async XLA Ops:
  0.6 1.6 %copy-start = (bf16[16,2,128,256]{3,2,1,0:T(8,128)(2,1)S(1)}, bf16[16,2,128,256]{3,2,1,0:T(8,128)(2,1)}, u32[]{:S(2)}) copy-start(bf16[16,2,128,256]{3,2,1,0:T(8,128)(2,1)} %refs_3_.3) | copy-start | bytes 6291460
  2.2 0.9 %copy-start.1 = (f32[256,256]{1,0:T(8,128)S(1)}, f32[256,256]{1,0:T(8,128)}, u32[]{:S(2)}) copy-start(f32[256,256]{1,0:T(8,128)} %refs_6_.1) | copy-start | bytes 786436
  3.2 0.7 %copy-start.2 = (s32[256]{0:T(256)S(1)}, s32[256]{0:T(256)}, u32[]{:S(2)}) copy-start(s32[256]{0:T(256)} %param.8) | copy-start | bytes 3076
  3.9 0.7 %copy-start.3 = (f32[2,128]{1,0:T(2,128)S(1)}, f32[2,128]{1,0:T(2,128)}, u32[]{:S(2)}) copy-start(f32[2,128]{1,0:T(2,128)} %refs_1_.3) | copy-start | bytes 3076
  4.5 0.7 %copy-start.4 = (f32[2,128]{1,0:T(2,128)S(1)}, f32[2,128]{1,0:T(2,128)}, u32[]{:S(2)}) copy-start(f32[2,128]{1,0:T(2,128)} %refs_2_.3) | copy-start | bytes 3076
  5.2 0.7 %copy-start.5 = (s32[8]{0:T(128)S(1)}, s32[8]{0:T(128)}, u32[]{:S(2)}) copy-start(s32[8]{0:T(128)} %refs_4_.1) | copy-start | bytes 100
  5.9 0.7 %copy-start.6 = (s32[128]{0:T(128)S(1)}, s32[128]{0:T(128)}, u32[]{:S(2)}) copy-start(s32[128]{0:T(128)} %param.10) | copy-start | bytes 1540
  9.9 3.1 %collective-permute-start = (bf16[128,16,128]{2,1,0:T(8,128)(2,1)S(1)}, bf16[128,16,128]{2,1,0:T(8,128)(2,1)S(1)}, u32[]{:S(2)}, u32[]{:S(2)}) collective-permute-start(bf16[128,16,128]{2,1,0:T(8,128)(2,1)S(1)} %get-tuple-element.29), channel_id=1, source_target_pairs={{0,1},{1,0},{2,3},{3,2},{4,5},{5,4},{6,7},{7,6},{8,9},{9,8},{10,11... | collective-permute-start | bytes 1572872 | tf_op jit(solution)/shard_map/ppermute | solution.py:393
  10.5 36.6 %copy-start.7 = (f32[1,16]{1,0:T(1,128)S(1)}, f32[1,16]{1,0:T(1,128)}, u32[]{:S(2)}) copy-start(f32[1,16]{1,0:T(1,128)} %refs_18_.1) | copy-start | bytes 196
  12.9 3.3 %collective-permute-start.1 = (bf16[128,16,128]{2,1,0:T(8,128)(2,1)S(1)}, bf16[128,16,128]{2,1,0:T(8,128)(2,1)S(1)}, u32[]{:S(2)}, u32[]{:S(2)}) collective-permute-start(bf16[128,16,128]{2,1,0:T(8,128)(2,1)S(1)} %get-tuple-element.36), channel_id=1, source_target_pairs={{0,1},{1,0},{2,3},{3,2},{4,5},{5,4},{6,7},{7,6},{8,9},{9,8},{10,11... | collective-permute-start | bytes 1572872 | tf_op jit(solution)/shard_map/ppermute | solution.py:393
  13.1 8.3 %collective-permute-start.2 = (bf16[16,16,128]{2,1,0:T(8,128)(2,1)S(1)}, bf16[16,16,128]{2,1,0:T(8,128)(2,1)S(1)}, u32[]{:S(2)}, u32[]{:S(2)}) collective-permute-start(bf16[16,16,128]{2,1,0:T(8,128)(2,1)S(1)} %get-tuple-element.38), channel_id=1, source_target_pairs={{0,2},{2,0},{4,6},{6,4},{8,10},{10,8},{12,14},{14,12},{1,3},{3,1},... | collective-permute-start | bytes 196616 | tf_op jit(solution)/shard_map/ppermute | solution.py:400
  16.3 6.4 %collective-permute-start.3 = (bf16[16,16,128]{2,1,0:T(8,128)(2,1)S(1)}, bf16[16,16,128]{2,1,0:T(8,128)(2,1)S(1)}, u32[]{:S(2)}, u32[]{:S(2)}) collective-permute-start(bf16[16,16,128]{2,1,0:T(8,128)(2,1)S(1)} %get-tuple-element.39), channel_id=1, source_target_pairs={{0,2},{2,0},{4,6},{6,4},{8,10},{10,8},{12,14},{14,12},{1,3},{3,1},... | collective-permute-start | bytes 196616 | tf_op jit(solution)/shard_map/ppermute | solution.py:400
  17.7 7.6 %collective-permute-start.4 = (bf16[16,16,128]{2,1,0:T(8,128)(2,1)S(1)}, bf16[16,16,128]{2,1,0:T(8,128)(2,1)S(1)}, u32[]{:S(2)}, u32[]{:S(2)}) collective-permute-start(bf16[16,16,128]{2,1,0:T(8,128)(2,1)S(1)} %get-tuple-element.40), channel_id=1, source_target_pairs={{0,4},{2,6},{4,0},{6,2},{8,12},{10,14},{12,8},{14,10},{1,5},{3,7},... | collective-permute-start | bytes 196616 | tf_op jit(solution)/shard_map/ppermute | solution.py:400
  19.3 6.3 %collective-permute-start.5 = (bf16[16,16,128]{2,1,0:T(8,128)(2,1)S(1)}, bf16[16,16,128]{2,1,0:T(8,128)(2,1)S(1)}, u32[]{:S(2)}, u32[]{:S(2)}) collective-permute-start(bf16[16,16,128]{2,1,0:T(8,128)(2,1)S(1)} %get-tuple-element.41), channel_id=1, source_target_pairs={{0,4},{2,6},{4,0},{6,2},{8,12},{10,14},{12,8},{14,10},{1,5},{3,7},... | collective-permute-start | bytes 196616 | tf_op jit(solution)/shard_map/ppermute | solution.py:400
  19.7 8.6 %collective-permute-start.6 = (bf16[16,16,128]{2,1,0:T(8,128)(2,1)S(1)}, bf16[16,16,128]{2,1,0:T(8,128)(2,1)S(1)}, u32[]{:S(2)}, u32[]{:S(2)}) collective-permute-start(bf16[16,16,128]{2,1,0:T(8,128)(2,1)S(1)} %get-tuple-element.42), channel_id=1, source_target_pairs={{0,6},{2,4},{4,2},{6,0},{8,14},{10,12},{12,10},{14,8},{1,7},{3,5},... | collective-permute-start | bytes 196616 | tf_op jit(solution)/shard_map/ppermute | solution.py:400
  21.4 8.0 %collective-permute-start.7 = (bf16[16,16,128]{2,1,0:T(8,128)(2,1)S(1)}, bf16[16,16,128]{2,1,0:T(8,128)(2,1)S(1)}, u32[]{:S(2)}, u32[]{:S(2)}) collective-permute-start(bf16[16,16,128]{2,1,0:T(8,128)(2,1)S(1)} %get-tuple-element.43), channel_id=1, source_target_pairs={{0,6},{2,4},{4,2},{6,0},{8,14},{10,12},{12,10},{14,8},{1,7},{3,5},... | collective-permute-start | bytes 196616 | tf_op jit(solution)/shard_map/ppermute | solution.py:400
  22.7 11.2 %collective-permute-start.8 = (bf16[16,16,128]{2,1,0:T(8,128)(2,1)S(1)}, bf16[16,16,128]{2,1,0:T(8,128)(2,1)S(1)}, u32[]{:S(2)}, u32[]{:S(2)}) collective-permute-start(bf16[16,16,128]{2,1,0:T(8,128)(2,1)S(1)} %get-tuple-element.44), channel_id=1, source_target_pairs={{0,8},{2,10},{4,12},{6,14},{8,0},{10,2},{12,4},{14,6},{1,9},{3,11}... | collective-permute-start | bytes 196616 | tf_op jit(solution)/shard_map/ppermute | solution.py:400
  25.3 12.7 %collective-permute-start.9 = (bf16[16,16,128]{2,1,0:T(8,128)(2,1)S(1)}, bf16[16,16,128]{2,1,0:T(8,128)(2,1)S(1)}, u32[]{:S(2)}, u32[]{:S(2)}) collective-permute-start(bf16[16,16,128]{2,1,0:T(8,128)(2,1)S(1)} %get-tuple-element.45), channel_id=1, source_target_pairs={{0,8},{2,10},{4,12},{6,14},{8,0},{10,2},{12,4},{14,6},{1,9},{3,11}... | collective-permute-start | bytes 196616 | tf_op jit(solution)/shard_map/ppermute | solution.py:400
  25.6 14.4 %collective-permute-start.10 = (bf16[16,16,128]{2,1,0:T(8,128)(2,1)S(1)}, bf16[16,16,128]{2,1,0:T(8,128)(2,1)S(1)}, u32[]{:S(2)}, u32[]{:S(2)}) collective-permute-start(bf16[16,16,128]{2,1,0:T(8,128)(2,1)S(1)} %get-tuple-element.46), channel_id=1, source_target_pairs={{0,10},{2,8},{4,14},{6,12},{8,2},{10,0},{12,6},{14,4},{1,11},{3,9}... | collective-permute-start | bytes 196616 | tf_op jit(solution)/shard_map/ppermute | solution.py:400
  28.3 14.9 %collective-permute-start.11 = (bf16[16,16,128]{2,1,0:T(8,128)(2,1)S(1)}, bf16[16,16,128]{2,1,0:T(8,128)(2,1)S(1)}, u32[]{:S(2)}, u32[]{:S(2)}) collective-permute-start(bf16[16,16,128]{2,1,0:T(8,128)(2,1)S(1)} %get-tuple-element.47), channel_id=1, source_target_pairs={{0,10},{2,8},{4,14},{6,12},{8,2},{10,0},{12,6},{14,4},{1,11},{3,9}... | collective-permute-start | bytes 196616 | tf_op jit(solution)/shard_map/ppermute | solution.py:400
  29.4 13.8 %collective-permute-start.12 = (bf16[16,16,128]{2,1,0:T(8,128)(2,1)S(1)}, bf16[16,16,128]{2,1,0:T(8,128)(2,1)S(1)}, u32[]{:S(2)}, u32[]{:S(2)}) collective-permute-start(bf16[16,16,128]{2,1,0:T(8,128)(2,1)S(1)} %get-tuple-element.48), channel_id=1, source_target_pairs={{0,12},{2,14},{4,8},{6,10},{8,4},{10,6},{12,0},{14,2},{1,13},{3,15... | collective-permute-start | bytes 196616 | tf_op jit(solution)/shard_map/ppermute | solution.py:400
  33.8 9.4 %collective-permute-start.13 = (bf16[16,16,128]{2,1,0:T(8,128)(2,1)S(1)}, bf16[16,16,128]{2,1,0:T(8,128)(2,1)S(1)}, u32[]{:S(2)}, u32[]{:S(2)}) collective-permute-start(bf16[16,16,128]{2,1,0:T(8,128)(2,1)S(1)} %get-tuple-element.49), channel_id=1, source_target_pairs={{0,12},{2,14},{4,8},{6,10},{8,4},{10,6},{12,0},{14,2},{1,13},{3,15... | collective-permute-start | bytes 196616 | tf_op jit(solution)/shard_map/ppermute | solution.py:400
  38.0 7.0 %collective-permute-start.14 = (bf16[16,16,128]{2,1,0:T(8,128)(2,1)S(1)}, bf16[16,16,128]{2,1,0:T(8,128)(2,1)S(1)}, u32[]{:S(2)}, u32[]{:S(2)}) collective-permute-start(bf16[16,16,128]{2,1,0:T(8,128)(2,1)S(1)} %get-tuple-element.50), channel_id=1, source_target_pairs={{0,14},{2,12},{4,10},{6,8},{8,6},{10,4},{12,2},{14,0},{1,15},{3,13... | collective-permute-start | bytes 196616 | tf_op jit(solution)/shard_map/ppermute | solution.py:400
  40.0 7.1 %collective-permute-start.15 = (bf16[16,16,128]{2,1,0:T(8,128)(2,1)S(1)}, bf16[16,16,128]{2,1,0:T(8,128)(2,1)S(1)}, u32[]{:S(2)}, u32[]{:S(2)}) collective-permute-start(bf16[16,16,128]{2,1,0:T(8,128)(2,1)S(1)} %get-tuple-element.51), channel_id=1, source_target_pairs={{0,14},{2,12},{4,10},{6,8},{8,6},{10,4},{12,2},{14,0},{1,15},{3,13... | collective-permute-start | bytes 196616 | tf_op jit(solution)/shard_map/ppermute | solution.py:400

commit v3 on v2

--- a/solution.py
+++ b/solution.py
@@ -58,82 +58,53 @@
 
 def partial_kernel(freq_total, slots, first_step, *refs):
     if first_step == 0:
-        (
-            cells_ref,
-            size_ref,
-            slope_ref,
-            field_hbm,
-            blocks_ref,
-            channel_ref,
-            delay_hbm,
-            other_ref,
-            own_ref,
-            next_cos_ref,
-            next_sin_ref,
-            step_cos_ref,
-            step_sin_ref,
-            field_ref,
-            field_sem,
-            delay_ref,
-            delay_sem,
-            picked_ref,
-            law_ref,
-            rows_ref,
-        ) = refs
+        hbm, outs, scratch = refs[:7], refs[7:16], refs[16:]
+        field_hbm, *small_hbm = hbm
+        other_ref, own_ref, next_cos_ref, next_sin_ref, *kept = outs
+        step_cos_ref, step_sin_ref, pick_ref, k_real_ref, k_imag_ref = kept
+        field_ref, picked_ref, law_ref, rows_ref, field_sem, small_sem, *small = scratch
+        cells_ref, size_ref, slope_ref, channel_ref, delay_ref, blocks_ref = small
     else:
-        (
-            cells_ref,
-            size_ref,
-            slope_ref,
-            field_hbm,
-            cos_ref,
-            sin_ref,
-            step_cos_ref,
-            step_sin_ref,
-            other_ref,
-            own_ref,
-            field_ref,
-            field_sem,
-            picked_ref,
-            law_ref,
-            rows_ref,
-        ) = refs
+        field_hbm, cos_ref, sin_ref, *kept = refs[:8]
+        step_cos_ref, step_sin_ref, pick_ref, k_real_ref, k_imag_ref = kept
+        other_ref, own_ref = refs[8:10]
+        field_ref, picked_ref, law_ref, rows_ref, field_sem = refs[10:]
     field_copy = pltpu.make_async_copy(
         field_hbm.at[pl.ds(first_step * W_STEP, W_STEP)], field_ref, field_sem
     )
-    field_copy.start()
+    elements, sites = field_ref.shape[2:]
     if first_step == 0:
-        delay_copy = pltpu.make_async_copy(delay_hbm, delay_ref, delay_sem)
-        delay_copy.start()
-    group = lax.axis_index("elem")
-    other = 1 - group
-    first_freq = lax.axis_index("freq") * W_DEV
-    elements, sites = field_ref.shape[2:]
-
-    order = slot_order(FG // slots, slots)
-    order_sel = order.astype(jnp.bfloat16)
-    picks, sizes, turns = [], [], []
-    for which in (other, group):
-        cells = jnp.where(which == 0, cells_ref[:, :FG], cells_ref[:, FG:])
-        cell_sel = lax.broadcasted_iota(jnp.int32, (sites, FG), 0) == cells
-        picks.append(dot(order_sel, cell_sel.astype(jnp.bfloat16), ((1,), (1,))))
-        size = size_ref[pl.ds(which, 1), :]
-        turn = size * slope_ref[pl.ds(which, 1), :] * (1.0 / freq_total)
-        sizes.append(jnp.sum(jnp.where(order, size, 0.0), axis=1, keepdims=True))
-        turns.append(jnp.sum(jnp.where(order, turn, 0.0), axis=1, keepdims=True))
-    pick = jnp.concatenate(picks, axis=0).astype(jnp.bfloat16)
-    size = jnp.concatenate(sizes, axis=0)
-    turn = jnp.concatenate(turns, axis=0)
-    freq = (
-        first_freq
-        + first_step * W_STEP
-        + lax.broadcasted_iota(jnp.int32, (2 * FG, FG), 1)
-    )
-    sine, cosine = sincos_turns(turn * freq.astype(jnp.float32))
-    k_real = size * (1.0 + EDGE) * cosine
-    k_imag = size * (EDGE - 1.0) * sine
-
-    if first_step == 0:
+        copies = [
+            pltpu.make_async_copy(source, target, small_sem.at[i])
+            for i, (source, target) in enumerate(zip(small_hbm, small))
+        ]
+        for copy in copies:
+            copy.start()
+        field_copy.start()
+        group = lax.axis_index("elem")
+        other = 1 - group
+        first_freq = lax.axis_index("freq") * W_DEV
+        order = slot_order(FG // slots, slots)
+        order_sel = order.astype(jnp.bfloat16)
+        for copy in copies:
+            copy.wait()
+        sizes, turns = [], []
+        for k, which in enumerate((other, group)):
+            cells = jnp.where(which == 0, cells_ref[:, :FG], cells_ref[:, FG:])
+            cell_sel = lax.broadcasted_iota(jnp.int32, (sites, FG), 0) == cells
+            pick_ref[k * FG : (k + 1) * FG, :] = dot(
+                order_sel, cell_sel.astype(jnp.bfloat16), ((1,), (1,))
+            ).astype(jnp.bfloat16)
+            size = size_ref[pl.ds(which, 1), :]
+            turn = size * slope_ref[pl.ds(which, 1), :] * (1.0 / freq_total)
+            sizes.append(jnp.sum(jnp.where(order, size, 0.0), axis=1, keepdims=True))
+            turns.append(jnp.sum(jnp.where(order, turn, 0.0), axis=1, keepdims=True))
+        size = jnp.concatenate(sizes, axis=0)
+        turn = jnp.concatenate(turns, axis=0)
+        freq = first_freq + lax.broadcasted_iota(jnp.int32, (2 * FG, FG), 1)
+        sine, cosine = sincos_turns(turn * freq.astype(jnp.float32))
+        k_real_ref[...] = size * (1.0 + EDGE) * cosine
+        k_imag_ref[...] = size * (EDGE - 1.0) * sine
         lane = lax.broadcasted_iota(jnp.int32, (1, 2 * ROWS), 1)
         position = lane & (SB - 1)
         for j in range(2 * NB):
@@ -150,7 +121,6 @@
             .astype(jnp.float32)
             .T.astype(jnp.bfloat16)
         )
-        delay_copy.wait()
         rest = delay_ref[...]
         delays = None
         for _piece in range(3):
@@ -165,6 +135,7 @@
         step_sin_ref[...] = step_sin
         sine, cosine = sincos_turns(phase * first_freq.astype(jnp.float32))
     else:
+        field_copy.start()
         cosine = cos_ref[...]
         sine = sin_ref[...]
         step_cos = step_cos_ref[...]
@@ -191,7 +162,7 @@
     field_copy.wait()
     for w in range(W_STEP):
         picked_ref[w] = dot(
-            pick, field_ref[w].reshape(2 * elements, sites), ((1,), (1,))
+            pick_ref[...], field_ref[w].reshape(2 * elements, sites), ((1,), (1,))
         ).astype(jnp.bfloat16)
     for k, out_ref in enumerate((other_ref, own_ref)):
         rows = slice(k * FG, (k + 1) * FG)
@@ -199,8 +170,9 @@
             product = dot(picked_ref[w, rows, :], law_ref[w, k], ((1,), (0,)))
             real_part = product[:, :ROWS]
             imag_part = product[:, ROWS:]
-            kr = k_real[rows, w : w + 1]
-            ki = k_imag[rows, w : w + 1]
+            freq = first_step * W_STEP + w
+            kr = k_real_ref[rows, freq : freq + 1]
+            ki = k_imag_ref[rows, freq : freq + 1]
             rows_ref[k, pl.ds(2 * w, FG, stride=2 * W_STEP), :] = (
                 kr * real_part - ki * imag_part
             )
@@ -212,30 +184,32 @@
         )
 
 
-def partials(small, field, extra, freq_total, slots, first_step):
+def partials(field, others, freq_total, slots, first_step):
     elements, sites = field.shape[2:]
     vmem = pl.BlockSpec(memory_space=pltpu.VMEM)
     hbm = pl.BlockSpec(memory_space=pltpu.HBM)
-    smem = pl.BlockSpec(memory_space=pltpu.SMEM)
     out_shape = [jax.ShapeDtypeStruct((FG, 2 * W_STEP, ROWS), jnp.bfloat16)] * 2
     scratch = [
         pltpu.VMEM((W_STEP, 2, elements, sites), jnp.bfloat16),
+        pltpu.VMEM((W_STEP, 2 * FG, 2 * elements), jnp.bfloat16),
+        pltpu.VMEM((W_STEP, 2, 2 * elements, 2 * ROWS), jnp.bfloat16),
+        pltpu.VMEM((2, FG * 2 * W_STEP, ROWS), jnp.float32),
         pltpu.SemaphoreType.DMA,
     ]
     if first_step == 0:
-        extra_specs = [smem, vmem, hbm]
         out_shape += [jax.ShapeDtypeStruct((elements, 2 * ROWS), jnp.float32)] * 4
-        scratch += [pltpu.VMEM(extra[2].shape, jnp.float32), pltpu.SemaphoreType.DMA]
+        out_shape += [jax.ShapeDtypeStruct((2 * FG, sites), jnp.bfloat16)]
+        out_shape += [jax.ShapeDtypeStruct((2 * FG, FG), jnp.float32)] * 2
+        scratch += [pltpu.SemaphoreType.DMA((len(others),))]
+        scratch += [pltpu.VMEM(a.shape, a.dtype) for a in others[:-1]]
+        scratch += [pltpu.SMEM(others[-1].shape, others[-1].dtype)]
+        others = [pltpu.with_memory_space_constraint(a, pltpu.HBM) for a in others]
+        specs = [hbm] * len(others)
     else:
-        extra_specs = [vmem] * 4
-    scratch += [
-        pltpu.VMEM((W_STEP, 2 * FG, 2 * elements), jnp.bfloat16),
-        pltpu.VMEM((W_STEP, 2, 2 * elements, 2 * ROWS), jnp.bfloat16),
-        pltpu.VMEM((2, FG * 2 * W_STEP, ROWS), jnp.float32),
-    ]
+        specs = [vmem] * len(others)
     return pl.pallas_call(
         functools.partial(partial_kernel, freq_total, slots, first_step),
-        in_specs=[vmem] * 3 + [hbm] + extra_specs,
+        in_specs=[hbm] + specs,
         out_specs=[vmem] * len(out_shape),
         out_shape=out_shape,
         scratch_shapes=scratch,
@@ -244,7 +218,7 @@
             flops=2 * W_STEP * 2 * 256**3, bytes_accessed=3 << 20, transcendentals=0
         ),
         name=f"partials_{first_step}",
-    )(*small, field, *extra)
+    )(pltpu.with_memory_space_constraint(field, pltpu.HBM), *others)
 
 
 def add_kernel(own_ref, moved_ref, *out_refs):
@@ -384,21 +358,28 @@
     sample_count = min(T_CAP, 2 * freq_total)
     swap = [(0, 1), (1, 0)]
     slots = freq_count if freq_count <= MOST_SLOTS else 1
-    small = (flaw_cells.reshape(1, -1), flaw_size, flaw_slope)
-    extra = (flaw_blocks, element_channel.reshape(1, -1), focal_delay)
+    others = (
+        flaw_cells.reshape(1, -1),
+        flaw_size,
+        flaw_slope,
+        element_channel.reshape(1, -1),
+        focal_delay,
+        flaw_blocks,
+    )
     chunks = []
     for first_step in range(W_DEV // W_STEP):
-        other, own, *state = partials(small, beam_field, extra, freq_total, slots, first_step)
-        extra = state if state else extra
+        other, own, *others = partials(beam_field, others, freq_total, slots, first_step)
         chunks.append(add(own, lax.ppermute(other, "elem", swap), slots))
     high, low = table(freq_total, slots, sample_count, 256 if freq_total <= 128 else 128)
     if slots > 1:
-        spectra = []
-        for slot in range(slots):
-            pairs = [(a, a ^ slot) for a in range(slots)]
-            for chunk in chunks:
-                moved = lax.ppermute(chunk[slot], "freq", pairs) if slot else chunk[slot]
-                spectra.append(moved[None])
+        spectra = {}
+        half = slots // 2
+        for chunk, arrays in enumerate(chunks):
+            for slot in [*range(half, slots), *range(1, half)]:
+                pairs = [(a, a ^ slot) for a in range(slots)]
+                spectra[slot, chunk] = lax.ppermute(arrays[slot], "freq", pairs)
+            spectra[0, chunk] = arrays[0]
+        spectra = [spectra[key][None] for key in sorted(spectra)]
     else:
         moved = lax.all_to_all(
             jnp.concatenate([chunk[0] for chunk in chunks], axis=1),

time: 49.3 us -> 43.5 us (0.88)
  local copies, waits for them, and re-layouts: 5.88 us -> 0.01 us
    unnamed x16 -> x2, local copies, waits for them, and re-layouts: 5.88 us -> 0.01 us
  transfers between devices with their start and end apart: 16 -> 16, of which waited for: 3 -> 3; matrix products, arithmetic and copies ran while one was open for 0% -> 0% of each run, Pallas kernels for 7% -> 8%
where the time goes in v3:
time: 43.5 us; the launch traced here: 43.3 us
  starting transfers between devices  29.2 us (67%)
  Pallas kernels  8.73 us (20%)
  waiting for transfers between devices  4.68 us (11%)
  between operations  0.7 us (2%)
    ppermute x14, starting transfers between devices, body(): spectra[slot, chunk] = lax.ppermute(arrays[slot], 'freq', pairs)  28.6 us
    pallas_call x2, Pallas kernels, partials(): pl.pallas_call(functools.partial(partial_kernel, freq_total, slots, first...  6.02 us
    ppermute x14, waiting for transfers between devices, body(): spectra[slot, chunk] = lax.ppermute(arrays[slot], 'freq', pairs)  4.67 us
    pallas_call x1, Pallas kernels, peaks(): pl.pallas_call(functools.partial(peak_kernel, freq_total, len(spectra)),...  1.92 us
  transfers between devices with their start and end apart: 16, of which 3 were waited for; matrix products, arithmetic and copies ran while one was open for 0% of the time, Pallas kernels for 8%

profile of v3, /device:TPU:0, one launch (start us, length us, event | category | flops | bytes accessed | tf_op | source)
XLA Modules:
  0.0 43.3 jit_solution(14507106687418215974)
XLA Ops:
  0.6 3.5 %partials_0.1 = (bf16[128,16,128]{2,1,0:T(8,128)(2,1)S(1)}, bf16[128,16,128]{2,1,0:T(8,128)(2,1)S(1)}, f32[128,256]{1,0:T(8,128)S(1)}, f32[128,256]{1,0:T(8,128)...) custom-call(bf16[16,2,128,256]{3,2,1,0:T(8,128)(2,1)} %refs_0_.3, ...), custom_call_target="tpu_custom_call" | custom-call | flops 536870912 | bytes 3145728 | tf_op jit(solution)/shard_map/partials_0/pallas_call | solution.py:210
  4.1 0.5 %collective-permute-start = (bf16[128,16,128]{2,1,0:T(8,128)(2,1)S(1)}, bf16[128,16,128]{2,1,0:T(8,128)(2,1)S(1)}, u32[]{:S(2)}, u32[]{:S(2)}) collective-permute-start(bf16[128,16,128]{2,1,0:T(8,128)(2,1)S(1)} %get-tuple-element.32), channel_id=1, source_target_pairs={{0,1},{1,0},{2,3},{3,2},{4,5},{5,4},{6,7},{7,6},{8,9},{9,8},{10,11... | collective-permute-start | bytes 1572872 | tf_op jit(solution)/shard_map/ppermute | solution.py:372
  4.7 0.0 copy-start
  4.7 2.5 %partials_1.1 = (bf16[128,16,128]{2,1,0:T(8,128)(2,1)S(1)}, bf16[128,16,128]{2,1,0:T(8,128)(2,1)S(1)}) custom-call(bf16[16,2,128,256]{3,2,1,0:T(8,128)(2,1)} %refs_0_.3, f32[128,256]{1,0:T(8,128)S(1)} %get-tuple-element.34.refs_1_, f32[128,256]{1,0:T(8,128)S(1)} %get-tuple-element.35.refs_2_, f32[128,256]{1,0:T(8,128)S(1)} %get-tuple-element.36.refs_3_, ...), custom_call_target="tpu_custom_call" | custom-call | flops 536870912 | bytes 3145728 | tf_op jit(solution)/shard_map/partials_1/pallas_call | solution.py:210
  7.2 0.1 collective-permute-start.1
  7.3 0.0 collective-permute-done.moved_ref
  7.3 0.1 add_groups.2
  7.4 3.0 %collective-permute-start.2 = (bf16[16,16,128]{2,1,0:T(8,128)(2,1)S(1)}, bf16[16,16,128]{2,1,0:T(8,128)(2,1)S(1)}, u32[]{:S(2)}, u32[]{:S(2)}) collective-permute-start(bf16[16,16,128]{2,1,0:T(8,128)(2,1)S(1)} %get-tuple-element.44), channel_id=1, source_target_pairs={{0,2},{2,0},{4,6},{6,4},{8,10},{10,8},{12,14},{14,12},{1,3},{3,1},... | collective-permute-start | bytes 196616 | tf_op jit(solution)/shard_map/ppermute | solution.py:380
  10.4 0.0 collective-permute-done.1.moved_ref
  10.5 0.1 add_groups.3
  10.6 1.4 %collective-permute-start.3 = (bf16[16,16,128]{2,1,0:T(8,128)(2,1)S(1)}, bf16[16,16,128]{2,1,0:T(8,128)(2,1)S(1)}, u32[]{:S(2)}, u32[]{:S(2)}) collective-permute-start(bf16[16,16,128]{2,1,0:T(8,128)(2,1)S(1)} %get-tuple-element.45), channel_id=1, source_target_pairs={{0,2},{2,0},{4,6},{6,4},{8,10},{10,8},{12,14},{14,12},{1,3},{3,1},... | collective-permute-start | bytes 196616 | tf_op jit(solution)/shard_map/ppermute | solution.py:380
  12.0 1.6 %collective-permute-start.4 = (bf16[16,16,128]{2,1,0:T(8,128)(2,1)S(1)}, bf16[16,16,128]{2,1,0:T(8,128)(2,1)S(1)}, u32[]{:S(2)}, u32[]{:S(2)}) collective-permute-start(bf16[16,16,128]{2,1,0:T(8,128)(2,1)S(1)} %get-tuple-element.46), channel_id=1, source_target_pairs={{0,4},{2,6},{4,0},{6,2},{8,12},{10,14},{12,8},{14,10},{1,5},{3,7},... | collective-permute-start | bytes 196616 | tf_op jit(solution)/shard_map/ppermute | solution.py:380
  13.6 0.4 %collective-permute-start.5 = (bf16[16,16,128]{2,1,0:T(8,128)(2,1)S(1)}, bf16[16,16,128]{2,1,0:T(8,128)(2,1)S(1)}, u32[]{:S(2)}, u32[]{:S(2)}) collective-permute-start(bf16[16,16,128]{2,1,0:T(8,128)(2,1)S(1)} %get-tuple-element.47), channel_id=1, source_target_pairs={{0,4},{2,6},{4,0},{6,2},{8,12},{10,14},{12,8},{14,10},{1,5},{3,7},... | collective-permute-start | bytes 196616 | tf_op jit(solution)/shard_map/ppermute | solution.py:380
  14.0 1.7 %collective-permute-start.6 = (bf16[16,16,128]{2,1,0:T(8,128)(2,1)S(1)}, bf16[16,16,128]{2,1,0:T(8,128)(2,1)S(1)}, u32[]{:S(2)}, u32[]{:S(2)}) collective-permute-start(bf16[16,16,128]{2,1,0:T(8,128)(2,1)S(1)} %get-tuple-element.48), channel_id=1, source_target_pairs={{0,6},{2,4},{4,2},{6,0},{8,14},{10,12},{12,10},{14,8},{1,7},{3,5},... | collective-permute-start | bytes 196616 | tf_op jit(solution)/shard_map/ppermute | solution.py:380
  15.7 0.0 collective-permute-done.2
  15.7 1.2 %collective-permute-start.7 = (bf16[16,16,128]{2,1,0:T(8,128)(2,1)S(1)}, bf16[16,16,128]{2,1,0:T(8,128)(2,1)S(1)}, u32[]{:S(2)}, u32[]{:S(2)}) collective-permute-start(bf16[16,16,128]{2,1,0:T(8,128)(2,1)S(1)} %get-tuple-element.49), channel_id=1, source_target_pairs={{0,6},{2,4},{4,2},{6,0},{8,14},{10,12},{12,10},{14,8},{1,7},{3,5},... | collective-permute-start | bytes 196616 | tf_op jit(solution)/shard_map/ppermute | solution.py:380
  17.0 0.0 collective-permute-done.3
  17.0 2.6 %collective-permute-start.8 = (bf16[16,16,128]{2,1,0:T(8,128)(2,1)S(1)}, bf16[16,16,128]{2,1,0:T(8,128)(2,1)S(1)}, u32[]{:S(2)}, u32[]{:S(2)}) collective-permute-start(bf16[16,16,128]{2,1,0:T(8,128)(2,1)S(1)} %get-tuple-element.50), channel_id=1, source_target_pairs={{0,8},{2,10},{4,12},{6,14},{8,0},{10,2},{12,4},{14,6},{1,9},{3,11}... | collective-permute-start | bytes 196616 | tf_op jit(solution)/shard_map/ppermute | solution.py:380
  19.5 0.0 collective-permute-done.4
  19.6 0.3 collective-permute-start.9
  19.9 0.0 collective-permute-done.5
  19.9 2.7 %collective-permute-start.10 = (bf16[16,16,128]{2,1,0:T(8,128)(2,1)S(1)}, bf16[16,16,128]{2,1,0:T(8,128)(2,1)S(1)}, u32[]{:S(2)}, u32[]{:S(2)}) collective-permute-start(bf16[16,16,128]{2,1,0:T(8,128)(2,1)S(1)} %get-tuple-element.52), channel_id=1, source_target_pairs={{0,10},{2,8},{4,14},{6,12},{8,2},{10,0},{12,6},{14,4},{1,11},{3,9}... | collective-permute-start | bytes 196616 | tf_op jit(solution)/shard_map/ppermute | solution.py:380
  22.6 0.0 collective-permute-done.6
  22.6 1.1 %collective-permute-start.11 = (bf16[16,16,128]{2,1,0:T(8,128)(2,1)S(1)}, bf16[16,16,128]{2,1,0:T(8,128)(2,1)S(1)}, u32[]{:S(2)}, u32[]{:S(2)}) collective-permute-start(bf16[16,16,128]{2,1,0:T(8,128)(2,1)S(1)} %get-tuple-element.53), channel_id=1, source_target_pairs={{0,10},{2,8},{4,14},{6,12},{8,2},{10,0},{12,6},{14,4},{1,11},{3,9}... | collective-permute-start | bytes 196616 | tf_op jit(solution)/shard_map/ppermute | solution.py:380
  23.7 0.0 collective-permute-done.7
  23.7 3.6 %collective-permute-start.12 = (bf16[16,16,128]{2,1,0:T(8,128)(2,1)S(1)}, bf16[16,16,128]{2,1,0:T(8,128)(2,1)S(1)}, u32[]{:S(2)}, u32[]{:S(2)}) collective-permute-start(bf16[16,16,128]{2,1,0:T(8,128)(2,1)S(1)} %get-tuple-element.54), channel_id=1, source_target_pairs={{0,12},{2,14},{4,8},{6,10},{8,4},{10,6},{12,0},{14,2},{1,13},{3,15... | collective-permute-start | bytes 196616 | tf_op jit(solution)/shard_map/ppermute | solution.py:380
  27.3 0.8 %collective-permute-done.8 = bf16[16,16,128]{2,1,0:T(8,128)(2,1)S(1)} collective-permute-done((bf16[16,16,128]{2,1,0:T(8,128)(2,1)S(1)}, bf16[16,16,128]{2,1,0:T(8,128)(2,1)S(1)}, u32[]{:S(2)}, u32[]{:S(2)}) %collective-permute-start.8) | collective-permute-done | bytes 65568 | tf_op jit(solution)/shard_map/ppermute | solution.py:380
  28.1 4.1 %collective-permute-start.13 = (bf16[16,16,128]{2,1,0:T(8,128)(2,1)S(1)}, bf16[16,16,128]{2,1,0:T(8,128)(2,1)S(1)}, u32[]{:S(2)}, u32[]{:S(2)}) collective-permute-start(bf16[16,16,128]{2,1,0:T(8,128)(2,1)S(1)} %get-tuple-element.55), channel_id=1, source_target_pairs={{0,12},{2,14},{4,8},{6,10},{8,4},{10,6},{12,0},{14,2},{1,13},{3,15... | collective-permute-start | bytes 196616 | tf_op jit(solution)/shard_map/ppermute | solution.py:380
  32.3 0.0 collective-permute-done.9
  32.3 2.1 %collective-permute-start.14 = (bf16[16,16,128]{2,1,0:T(8,128)(2,1)S(1)}, bf16[16,16,128]{2,1,0:T(8,128)(2,1)S(1)}, u32[]{:S(2)}, u32[]{:S(2)}) collective-permute-start(bf16[16,16,128]{2,1,0:T(8,128)(2,1)S(1)} %get-tuple-element.56), channel_id=1, source_target_pairs={{0,14},{2,12},{4,10},{6,8},{8,6},{10,4},{12,2},{14,0},{1,15},{3,13... | collective-permute-start | bytes 196616 | tf_op jit(solution)/shard_map/ppermute | solution.py:380
  34.3 0.0 collective-permute-done.10
  34.3 2.7 %collective-permute-start.15 = (bf16[16,16,128]{2,1,0:T(8,128)(2,1)S(1)}, bf16[16,16,128]{2,1,0:T(8,128)(2,1)S(1)}, u32[]{:S(2)}, u32[]{:S(2)}) collective-permute-start(bf16[16,16,128]{2,1,0:T(8,128)(2,1)S(1)} %get-tuple-element.57), channel_id=1, source_target_pairs={{0,14},{2,12},{4,10},{6,8},{8,6},{10,4},{12,2},{14,0},{1,15},{3,13... | collective-permute-start | bytes 196616 | tf_op jit(solution)/shard_map/ppermute | solution.py:380
  37.0 0.5 %table.1 = (bf16[1,512,256]{2,1,0:T(8,128)(2,1)S(1)}, bf16[1,512,256]{2,1,0:T(8,128)(2,1)S(1)}) custom-call(), custom_call_target="tpu_custom_call" | custom-call | tf_op jit(solution)/shard_map/table/pallas_call | solution.py:269
  37.5 0.0 collective-permute-done.11
  37.5 0.0 collective-permute-done.12
  37.6 0.0 collective-permute-done.13
  37.6 1.7 %collective-permute-done.14 = bf16[16,16,128]{2,1,0:T(8,128)(2,1)S(1)} collective-permute-done((bf16[16,16,128]{2,1,0:T(8,128)(2,1)S(1)}, bf16[16,16,128]{2,1,0:T(8,128)(2,1)S(1)}, u32[]{:S(2)}, u32[]{:S(2)}) %collective-permute-start.14) | collective-permute-done | bytes 65568 | tf_op jit(solution)/shard_map/ppermute | solution.py:380
  39.2 2.1 %collective-permute-done.15 = bf16[16,16,128]{2,1,0:T(8,128)(2,1)S(1)} collective-permute-done((bf16[16,16,128]{2,1,0:T(8,128)(2,1)S(1)}, bf16[16,16,128]{2,1,0:T(8,128)(2,1)S(1)}, u32[]{:S(2)}, u32[]{:S(2)}) %collective-permute-start.15) | collective-permute-done | bytes 65568 | tf_op jit(solution)/shard_map/ppermute | solution.py:380
  41.4 0.0 copy-done
  41.4 1.9 %peaks.1 = (f32[1,16]{1,0:T(1,128)}, f32[1,16]{1,0:T(1,128)}) custom-call(bf16[1,16,16,128]{3,2,1,0:T(8,128)(2,1)S(1)} %bitcast.18, bf16[1,16,16,128]{3,2,1,0:T(8,128)(2,1)S(1)} %bitcast.20, bf16[1,16,16,128]{3,2,1,0:T(8,128)(2,1)S(1)} %bitcast.19, bf16[1,16,16,128]{3,2,1,0:T(8,128)(2,1)S(1)} %bitcast.21, bf16[1,16,16,128]{3,2,1,0:T(8,128)(2,1)S(1)} %bitcast.22, ...), custom_call_target="tpu_custom_call" | custom-call | tf_op jit(solution)/shard_map/peaks/pallas_call | solution.py:333
Async XLA Ops:
  4.1 3.2 %collective-permute-start = (bf16[128,16,128]{2,1,0:T(8,128)(2,1)S(1)}, bf16[128,16,128]{2,1,0:T(8,128)(2,1)S(1)}, u32[]{:S(2)}, u32[]{:S(2)}) collective-permute-start(bf16[128,16,128]{2,1,0:T(8,128)(2,1)S(1)} %get-tuple-element.32), channel_id=1, source_target_pairs={{0,1},{1,0},{2,3},{3,2},{4,5},{5,4},{6,7},{7,6},{8,9},{9,8},{10,11... | collective-permute-start | bytes 1572872 | tf_op jit(solution)/shard_map/ppermute | solution.py:372
  4.7 36.7 %copy-start = (f32[1,16]{1,0:T(1,128)S(1)}, f32[1,16]{1,0:T(1,128)}, u32[]{:S(2)}) copy-start(f32[1,16]{1,0:T(1,128)} %refs_18_.1) | copy-start | bytes 196
  7.2 3.3 %collective-permute-start.1 = (bf16[128,16,128]{2,1,0:T(8,128)(2,1)S(1)}, bf16[128,16,128]{2,1,0:T(8,128)(2,1)S(1)}, u32[]{:S(2)}, u32[]{:S(2)}) collective-permute-start(bf16[128,16,128]{2,1,0:T(8,128)(2,1)S(1)} %get-tuple-element.42), channel_id=1, source_target_pairs={{0,1},{1,0},{2,3},{3,2},{4,5},{5,4},{6,7},{7,6},{8,9},{9,8},{10,11... | collective-permute-start | bytes 1572872 | tf_op jit(solution)/shard_map/ppermute | solution.py:372
  7.4 8.3 %collective-permute-start.2 = (bf16[16,16,128]{2,1,0:T(8,128)(2,1)S(1)}, bf16[16,16,128]{2,1,0:T(8,128)(2,1)S(1)}, u32[]{:S(2)}, u32[]{:S(2)}) collective-permute-start(bf16[16,16,128]{2,1,0:T(8,128)(2,1)S(1)} %get-tuple-element.44), channel_id=1, source_target_pairs={{0,2},{2,0},{4,6},{6,4},{8,10},{10,8},{12,14},{14,12},{1,3},{3,1},... | collective-permute-start | bytes 196616 | tf_op jit(solution)/shard_map/ppermute | solution.py:380
  10.6 6.4 %collective-permute-start.3 = (bf16[16,16,128]{2,1,0:T(8,128)(2,1)S(1)}, bf16[16,16,128]{2,1,0:T(8,128)(2,1)S(1)}, u32[]{:S(2)}, u32[]{:S(2)}) collective-permute-start(bf16[16,16,128]{2,1,0:T(8,128)(2,1)S(1)} %get-tuple-element.45), channel_id=1, source_target_pairs={{0,2},{2,0},{4,6},{6,4},{8,10},{10,8},{12,14},{14,12},{1,3},{3,1},... | collective-permute-start | bytes 196616 | tf_op jit(solution)/shard_map/ppermute | solution.py:380
  12.0 7.6 %collective-permute-start.4 = (bf16[16,16,128]{2,1,0:T(8,128)(2,1)S(1)}, bf16[16,16,128]{2,1,0:T(8,128)(2,1)S(1)}, u32[]{:S(2)}, u32[]{:S(2)}) collective-permute-start(bf16[16,16,128]{2,1,0:T(8,128)(2,1)S(1)} %get-tuple-element.46), channel_id=1, source_target_pairs={{0,4},{2,6},{4,0},{6,2},{8,12},{10,14},{12,8},{14,10},{1,5},{3,7},... | collective-permute-start | bytes 196616 | tf_op jit(solution)/shard_map/ppermute | solution.py:380
  13.6 6.3 %collective-permute-start.5 = (bf16[16,16,128]{2,1,0:T(8,128)(2,1)S(1)}, bf16[16,16,128]{2,1,0:T(8,128)(2,1)S(1)}, u32[]{:S(2)}, u32[]{:S(2)}) collective-permute-start(bf16[16,16,128]{2,1,0:T(8,128)(2,1)S(1)} %get-tuple-element.47), channel_id=1, source_target_pairs={{0,4},{2,6},{4,0},{6,2},{8,12},{10,14},{12,8},{14,10},{1,5},{3,7},... | collective-permute-start | bytes 196616 | tf_op jit(solution)/shard_map/ppermute | solution.py:380
  14.0 8.6 %collective-permute-start.6 = (bf16[16,16,128]{2,1,0:T(8,128)(2,1)S(1)}, bf16[16,16,128]{2,1,0:T(8,128)(2,1)S(1)}, u32[]{:S(2)}, u32[]{:S(2)}) collective-permute-start(bf16[16,16,128]{2,1,0:T(8,128)(2,1)S(1)} %get-tuple-element.48), channel_id=1, source_target_pairs={{0,6},{2,4},{4,2},{6,0},{8,14},{10,12},{12,10},{14,8},{1,7},{3,5},... | collective-permute-start | bytes 196616 | tf_op jit(solution)/shard_map/ppermute | solution.py:380
  15.7 8.0 %collective-permute-start.7 = (bf16[16,16,128]{2,1,0:T(8,128)(2,1)S(1)}, bf16[16,16,128]{2,1,0:T(8,128)(2,1)S(1)}, u32[]{:S(2)}, u32[]{:S(2)}) collective-permute-start(bf16[16,16,128]{2,1,0:T(8,128)(2,1)S(1)} %get-tuple-element.49), channel_id=1, source_target_pairs={{0,6},{2,4},{4,2},{6,0},{8,14},{10,12},{12,10},{14,8},{1,7},{3,5},... | collective-permute-start | bytes 196616 | tf_op jit(solution)/shard_map/ppermute | solution.py:380
  17.0 11.2 %collective-permute-start.8 = (bf16[16,16,128]{2,1,0:T(8,128)(2,1)S(1)}, bf16[16,16,128]{2,1,0:T(8,128)(2,1)S(1)}, u32[]{:S(2)}, u32[]{:S(2)}) collective-permute-start(bf16[16,16,128]{2,1,0:T(8,128)(2,1)S(1)} %get-tuple-element.50), channel_id=1, source_target_pairs={{0,8},{2,10},{4,12},{6,14},{8,0},{10,2},{12,4},{14,6},{1,9},{3,11}... | collective-permute-start | bytes 196616 | tf_op jit(solution)/shard_map/ppermute | solution.py:380
  19.6 12.7 %collective-permute-start.9 = (bf16[16,16,128]{2,1,0:T(8,128)(2,1)S(1)}, bf16[16,16,128]{2,1,0:T(8,128)(2,1)S(1)}, u32[]{:S(2)}, u32[]{:S(2)}) collective-permute-start(bf16[16,16,128]{2,1,0:T(8,128)(2,1)S(1)} %get-tuple-element.51), channel_id=1, source_target_pairs={{0,8},{2,10},{4,12},{6,14},{8,0},{10,2},{12,4},{14,6},{1,9},{3,11}... | collective-permute-start | bytes 196616 | tf_op jit(solution)/shard_map/ppermute | solution.py:380
  19.9 14.4 %collective-permute-start.10 = (bf16[16,16,128]{2,1,0:T(8,128)(2,1)S(1)}, bf16[16,16,128]{2,1,0:T(8,128)(2,1)S(1)}, u32[]{:S(2)}, u32[]{:S(2)}) collective-permute-start(bf16[16,16,128]{2,1,0:T(8,128)(2,1)S(1)} %get-tuple-element.52), channel_id=1, source_target_pairs={{0,10},{2,8},{4,14},{6,12},{8,2},{10,0},{12,6},{14,4},{1,11},{3,9}... | collective-permute-start | bytes 196616 | tf_op jit(solution)/shard_map/ppermute | solution.py:380
  22.6 14.9 %collective-permute-start.11 = (bf16[16,16,128]{2,1,0:T(8,128)(2,1)S(1)}, bf16[16,16,128]{2,1,0:T(8,128)(2,1)S(1)}, u32[]{:S(2)}, u32[]{:S(2)}) collective-permute-start(bf16[16,16,128]{2,1,0:T(8,128)(2,1)S(1)} %get-tuple-element.53), channel_id=1, source_target_pairs={{0,10},{2,8},{4,14},{6,12},{8,2},{10,0},{12,6},{14,4},{1,11},{3,9}... | collective-permute-start | bytes 196616 | tf_op jit(solution)/shard_map/ppermute | solution.py:380
  23.7 13.8 %collective-permute-start.12 = (bf16[16,16,128]{2,1,0:T(8,128)(2,1)S(1)}, bf16[16,16,128]{2,1,0:T(8,128)(2,1)S(1)}, u32[]{:S(2)}, u32[]{:S(2)}) collective-permute-start(bf16[16,16,128]{2,1,0:T(8,128)(2,1)S(1)} %get-tuple-element.54), channel_id=1, source_target_pairs={{0,12},{2,14},{4,8},{6,10},{8,4},{10,6},{12,0},{14,2},{1,13},{3,15... | collective-permute-start | bytes 196616 | tf_op jit(solution)/shard_map/ppermute | solution.py:380
  28.1 9.4 %collective-permute-start.13 = (bf16[16,16,128]{2,1,0:T(8,128)(2,1)S(1)}, bf16[16,16,128]{2,1,0:T(8,128)(2,1)S(1)}, u32[]{:S(2)}, u32[]{:S(2)}) collective-permute-start(bf16[16,16,128]{2,1,0:T(8,128)(2,1)S(1)} %get-tuple-element.55), channel_id=1, source_target_pairs={{0,12},{2,14},{4,8},{6,10},{8,4},{10,6},{12,0},{14,2},{1,13},{3,15... | collective-permute-start | bytes 196616 | tf_op jit(solution)/shard_map/ppermute | solution.py:380
  32.3 7.0 %collective-permute-start.14 = (bf16[16,16,128]{2,1,0:T(8,128)(2,1)S(1)}, bf16[16,16,128]{2,1,0:T(8,128)(2,1)S(1)}, u32[]{:S(2)}, u32[]{:S(2)}) collective-permute-start(bf16[16,16,128]{2,1,0:T(8,128)(2,1)S(1)} %get-tuple-element.56), channel_id=1, source_target_pairs={{0,14},{2,12},{4,10},{6,8},{8,6},{10,4},{12,2},{14,0},{1,15},{3,13... | collective-permute-start | bytes 196616 | tf_op jit(solution)/shard_map/ppermute | solution.py:380
  34.3 7.1 %collective-permute-start.15 = (bf16[16,16,128]{2,1,0:T(8,128)(2,1)S(1)}, bf16[16,16,128]{2,1,0:T(8,128)(2,1)S(1)}, u32[]{:S(2)}, u32[]{:S(2)}) collective-permute-start(bf16[16,16,128]{2,1,0:T(8,128)(2,1)S(1)} %get-tuple-element.57), channel_id=1, source_target_pairs={{0,14},{2,12},{4,10},{6,8},{8,6},{10,4},{12,2},{14,0},{1,15},{3,13... | collective-permute-start | bytes 196616 | tf_op jit(solution)/shard_map/ppermute | solution.py:380
